TPU v7x, 128 devices: a whole 4x4x4 slice. The times are simulated.
128 devices in a mesh: rep: 8 (over y, core), seq: 16 (over z, x).
Axes of the slice: x: 4, y: 4, z: 4, core: 2. Of those that a mesh axis runs over, the one named last changes fastest.
Arguments:
- tokens: bfloat16 [16384, 1536], P(('rep', 'seq')), may hold values from -24 to 24
- norm_gain: float32 [1536], replicated, may hold values from 0.5 to 1.5
- w_main: bfloat16 [1536, 6400], P('seq'), may hold values from -0.15625 to 0.15625
- w_dt: bfloat16 [1536, 48], P('seq'), may hold values from -0.078125 to 0.078125
- conv_weight: float32 [4, 3328], replicated, may hold values from -3 to 3
- conv_bias: float32 [3328], replicated, may hold values from -3 to 3
- dt_bias: float32 [48], replicated, as said below
- a_log: float32 [48], replicated, as said below
- skip_gain: float32 [48], replicated, may hold values from 0.5 to 1.5
- out_gain: float32 [3072], replicated, may hold values from 0.5 to 1.5
- w_out: bfloat16 [3072, 1536], P('seq'), may hold values from -0.109375 to 0.109375
- cotangent: bfloat16 [16384, 1536], P(('rep', 'seq')), may hold values from -6 to 6
Outputs:
- block_out: bfloat16 [16384, 1536], P(('rep', 'seq'))
- grad_tokens: bfloat16 [16384, 1536], P(('rep', 'seq'))
- grad_norm_gain: float32 [1536], replicated
- grad_w_main: float32 [1536, 6400], P('seq')
- grad_w_dt: float32 [1536, 48], P('seq')
- grad_conv_weight: float32 [4, 3328], replicated
- grad_conv_bias: float32 [3328], replicated
- grad_dt_bias: float32 [48], replicated
- grad_a_log: float32 [48], replicated
- grad_skip_gain: float32 [48], replicated
- grad_out_gain: float32 [3072], replicated
- grad_w_out: float32 [3072, 1536], P('seq')
Inputs may be any that keep to these rules, and one draw needn't show every extreme that they name: softplus(dt_bias) lies between 0.02 and 0.1 for every head. For every head, exp(a_log) * softplus(dt_bias) lies between 0.3 / 2048 and 0.04.
All inputs are finite; a program needn't handle non-finite values.
Results may differ from a plain program's by a relative error of at most 0.019.
Values may be sent and summed in bfloat16 or wider, within the bound.
No kernel may reach another device: no remote copies, remote signals or barrier semaphores. Data moves between devices by JAX's collectives and lax.ppermute only.
A program may use at most 192 MiB of HBM per device.

v0:
```python
import jax
import jax.numpy as jnp
from jax import lax
from jax.sharding import PartitionSpec as P

EPS = 1e-05
PRECISE = lax.Precision.HIGHEST


def from_behind(value, axis, steps):
    count = lax.axis_size(axis)
    leading, last = (max(0, -steps), min(count, count - steps))
    return lax.ppermute(value, axis, [(source, source + steps) for source in range(leading, last)])


def carried_in(array, axis, combine, identity):
    peers, mine = (lax.axis_size(axis), lax.axis_index(axis))
    everything = jax.tree.map(
        lambda part, kind: lax.all_gather(part.astype(kind), axis),
        array,
        (jnp.bfloat16, jnp.bfloat16),
    )
    start = jax.tree.map(
        lambda part, zero: jnp.broadcast_to(jnp.asarray(zero, part.dtype), part.shape),
        array,
        identity,
    )

    def step(k, before):
        reached = k < mine
        new = combine(
            before, jax.tree.map(lambda part, own: part[k].astype(own.dtype), everything, array)
        )
        return jax.tree.map(lambda a, b: jnp.where(reached, a, b), new, before)

    return lax.fori_loop(0, peers, step, start)


def entering_2(array, axis, join, neutral):
    count = lax.axis_size(axis)
    place = lax.axis_index(axis)
    ahead = count - 1 - place
    gathered = jax.tree.map(
        lambda a, kind: lax.all_gather(a.astype(kind), axis),
        array,
        jax.tree.map(lambda a: jnp.bfloat16 if a.dtype == jnp.float32 else a.dtype, array),
    )
    state = jax.tree.map(lambda a, e: jnp.zeros_like(a) + jnp.asarray(e, a.dtype), array, neutral)

    def one(step, state):
        source = count - 1 - step
        return join(
            state,
            jax.tree.map(
                lambda a, own: lax.dynamic_index_in_dim(a, source, 0, False).astype(own.dtype),
                gathered,
                array,
            ),
        )

    return lax.fori_loop(0, ahead, one, state)


def pre_norm(seq_tokens, norm_gain):
    inv_root = lax.rsqrt(jnp.mean(seq_tokens * seq_tokens, axis=-1, keepdims=True) + EPS)
    return seq_tokens * inv_root * norm_gain


def gated_norm(mixed_y, gate_branch, out_gain):
    gated = mixed_y * jax.nn.silu(gate_branch)
    inv_root = lax.rsqrt(jnp.mean(gated * gated, axis=-1, keepdims=True) + EPS)
    return gated * inv_root * out_gain


def causal_conv(extended, conv_weight, conv_bias):
    conv_width = conv_weight.shape[0]
    row_count = extended.shape[0] - conv_width + 1
    summed = conv_bias + extended[0:row_count] * conv_weight[0]
    for offset in range(1, conv_width):
        summed = summed + extended[offset : offset + row_count] * conv_weight[offset]
    return jax.nn.silu(summed)


def span_step(carry_state, inputs):
    block_values, block_write, block_read, block_dt, block_decay = inputs
    block_len = block_values.shape[0]
    log_growth = jnp.cumsum(block_decay, axis=0)
    causal = (
        lax.broadcasted_iota(jnp.int32, (block_len, block_len), 0)
        >= lax.broadcasted_iota(jnp.int32, (block_len, block_len), 1)
    )[:, :, None]
    spread = log_growth[:, None, :] - log_growth[None, :, :]
    decay_matrix = jnp.where(causal, jnp.exp(jnp.where(causal, spread, 0.0)), 0.0)
    scores = jnp.dot(block_read, block_write.T, precision=PRECISE)
    scaled_values = block_values * block_dt[:, :, None]
    outputs = jnp.einsum(
        "tsh,shp->thp", scores[:, :, None] * decay_matrix, scaled_values, precision=PRECISE
    )
    outputs = outputs + jnp.exp(log_growth)[:, :, None] * jnp.einsum(
        "tn,hpn->thp", block_read, carry_state, precision=PRECISE
    )
    last_log = log_growth[-1]
    tail_decay = jnp.exp(last_log[None, :] - log_growth)
    carry_state = jnp.exp(last_log)[:, None, None] * carry_state + jnp.einsum(
        "th,thp,tn->hpn", tail_decay, scaled_values, block_write, precision=PRECISE
    )
    return (carry_state, outputs)


def local_ssd(values, write_rows, read_rows, dt_raw, dt_bias, a_log, skip_gain):
    step_sizes = jax.nn.softplus(dt_raw + dt_bias)
    log_decay = -step_sizes * jnp.exp(a_log)
    row_count, head_count, head_size = values.shape
    block_len = min(256, row_count)
    block_count = row_count // block_len

    def split_blocks(member):
        return member.reshape((block_count, block_len) + member.shape[1:])

    start = jnp.zeros((head_count, head_size, write_rows.shape[1]), jnp.float32)
    final_state, outputs = lax.scan(
        span_step,
        start,
        (
            split_blocks(values),
            split_blocks(write_rows),
            split_blocks(read_rows),
            split_blocks(step_sizes),
            split_blocks(log_decay),
        ),
    )
    log_growth = jnp.cumsum(log_decay, axis=0)
    local_y = outputs.reshape(values.shape) + skip_gain[None, :, None] * values
    return (local_y, final_state, log_growth)


def combine_states(first_part, second_part):
    return (
        first_part[0] + second_part[0],
        jnp.exp(second_part[0])[:, None, None] * first_part[1] + second_part[1],
    )


def local(
    tokens,
    norm_gain,
    w_main,
    w_dt,
    conv_weight,
    conv_bias,
    dt_bias,
    a_log,
    skip_gain,
    out_gain,
    w_out,
    cotangent,
):
    head_count = a_log.shape[0]
    inner_width = out_gain.shape[0]
    head_size = inner_width // head_count
    state_size = (conv_weight.shape[1] - inner_width) // 2
    conv_width = conv_weight.shape[0]
    row_count = tokens.shape[0]
    full_main, full_dt, full_out = (
        lax.all_gather(w_main, "seq", axis=0, tiled=True),
        lax.all_gather(w_dt, "seq", axis=0, tiled=True),
        lax.all_gather(w_out, "seq", axis=0, tiled=True),
    )
    token_values = tokens.astype(jnp.float32)
    normed, norm_back = jax.vjp(pre_norm, token_values, norm_gain)
    normed_low = normed.astype(jnp.bfloat16)
    projected = jnp.dot(normed_low, full_main, preferred_element_type=jnp.float32)
    dt_raw = jnp.dot(normed_low, full_dt, preferred_element_type=jnp.float32)
    gate_branch = projected[:, :inner_width]
    conv_input = projected[:, inner_width:].astype(jnp.bfloat16)
    before = from_behind(conv_input[row_count - conv_width + 1 :], "seq", 1)
    extended = jnp.concatenate([before, conv_input], axis=0).astype(jnp.float32)
    activated, conv_back = jax.vjp(causal_conv, extended, conv_weight, conv_bias)
    act_low = activated.astype(jnp.bfloat16)
    values = act_low[:, :inner_width].astype(jnp.float32).reshape(row_count, head_count, head_size)
    write_rows = act_low[:, inner_width : inner_width + state_size].astype(jnp.float32)
    read_rows = act_low[:, inner_width + state_size :].astype(jnp.float32)
    (local_y, final_state, log_growth), ssd_back = jax.vjp(
        local_ssd, values, write_rows, read_rows, dt_raw, dt_bias, a_log, skip_gain
    )
    totals = log_growth[-1]
    identity = (jnp.zeros_like(totals), jnp.zeros_like(final_state))
    unused_total, entering = carried_in((totals, final_state), "seq", combine_states, identity)
    growth = jnp.exp(log_growth)
    carried = jnp.einsum("tn,hpn->thp", read_rows, entering, precision=PRECISE)
    mixed_y = local_y + growth[:, :, None] * carried
    normed_y, gate_back = jax.vjp(
        gated_norm, mixed_y.reshape(row_count, inner_width), gate_branch, out_gain
    )
    mixed_low = normed_y.astype(jnp.bfloat16)
    block_out = (
        token_values + jnp.dot(mixed_low, full_out, preferred_element_type=jnp.float32)
    ).astype(jnp.bfloat16)
    back_main, back_dt, back_out = (
        lax.all_gather(w_main, "seq", axis=0, tiled=True),
        lax.all_gather(w_dt, "seq", axis=0, tiled=True),
        lax.all_gather(w_out, "seq", axis=0, tiled=True),
    )
    grad_out_local = jnp.einsum(
        "ti,td->id", mixed_low, cotangent, preferred_element_type=jnp.float32
    )
    grad_normed_y = jnp.einsum("td,id->ti", cotangent, back_out, preferred_element_type=jnp.float32)
    grad_mixed, grad_gate, grad_out_gain = gate_back(grad_normed_y)
    grad_mixed = grad_mixed.reshape(row_count, head_count, head_size)
    weighted = growth[:, :, None] * grad_mixed
    read_extra = jnp.einsum("thp,hpn->tn", weighted, entering, precision=PRECISE)
    grad_growth = jnp.sum(weighted * carried, axis=2)
    state_pull = jnp.einsum("thp,tn->hpn", weighted, read_rows, precision=PRECISE)
    unused_back, leaving = entering_2((totals, state_pull), "seq", combine_states, identity)
    grad_totals = jnp.exp(totals) * jnp.sum(leaving * entering, axis=(1, 2))
    grad_growth = grad_growth.at[row_count - 1].add(grad_totals)
    grad_values, grad_write, grad_read, grad_dt_raw, grad_dt_bias, grad_a_log, grad_skip_gain = (
        ssd_back((grad_mixed, leaving, grad_growth))
    )
    grad_read = grad_read + read_extra
    grad_activated = jnp.concatenate(
        [grad_values.reshape(row_count, inner_width), grad_write, grad_read], axis=1
    )
    grad_extended, grad_conv_weight, grad_conv_bias = conv_back(grad_activated)
    spill_rows = from_behind(
        grad_extended[: conv_width - 1].astype(jnp.bfloat16), "seq", -1
    ).astype(jnp.float32)
    spill_full = jnp.concatenate(
        [jnp.zeros((row_count - conv_width + 1, spill_rows.shape[1]), jnp.float32), spill_rows],
        axis=0,
    )
    grad_conv_input = grad_extended[conv_width - 1 :] + spill_full
    grad_projected = jnp.concatenate([grad_gate, grad_conv_input], axis=1).astype(jnp.bfloat16)
    grad_dt_low = grad_dt_raw.astype(jnp.bfloat16)
    grad_main_local = jnp.einsum(
        "td,tc->dc", normed_low, grad_projected, preferred_element_type=jnp.float32
    )
    grad_dt_local = jnp.einsum(
        "td,th->dh", normed_low, grad_dt_low, preferred_element_type=jnp.float32
    )
    grad_normed = jnp.einsum(
        "tc,dc->td", grad_projected, back_main, preferred_element_type=jnp.float32
    ) + jnp.einsum("th,dh->td", grad_dt_low, back_dt, preferred_element_type=jnp.float32)
    grad_inputs, grad_norm_gain = norm_back(grad_normed)
    grad_tokens = (cotangent.astype(jnp.float32) + grad_inputs).astype(jnp.bfloat16)
    small_sums = lax.psum(
        (
            grad_norm_gain,
            grad_conv_weight,
            grad_conv_bias,
            grad_dt_bias,
            grad_a_log,
            grad_skip_gain,
            grad_out_gain,
        ),
        ("rep", "seq"),
    )
    shards = (
        lax.psum_scatter(
            grad_main_local.astype(jnp.bfloat16), "seq", scatter_dimension=0, tiled=True
        ).astype(jnp.float32),
        lax.psum_scatter(
            grad_dt_local.astype(jnp.bfloat16), "seq", scatter_dimension=0, tiled=True
        ).astype(jnp.float32),
        lax.psum_scatter(
            grad_out_local.astype(jnp.bfloat16), "seq", scatter_dimension=0, tiled=True
        ).astype(jnp.float32),
    )
    shards = (
        lax.psum(shards[0].astype(jnp.bfloat16), "rep").astype(jnp.float32),
        lax.psum(shards[1].astype(jnp.bfloat16), "rep").astype(jnp.float32),
        lax.psum(shards[2].astype(jnp.bfloat16), "rep").astype(jnp.float32),
    )
    return (
        block_out,
        grad_tokens,
        small_sums[0],
        shards[0],
        shards[1],
        small_sums[1],
        small_sums[2],
        small_sums[3],
        small_sums[4],
        small_sums[5],
        small_sums[6],
        shards[2],
    )


def solution(mesh):
    placed = (
        P(("rep", "seq"), None),
        P(),
        P("seq", None),
        P("seq", None),
        P(),
        P(),
        P(),
        P(),
        P(),
        P(),
        P("seq", None),
        P(("rep", "seq"), None),
    )
    return jax.shard_map(
        local,
        mesh=mesh,
        in_specs=placed,
        out_specs=(
            P(("rep", "seq"), None),
            P(("rep", "seq"), None),
            P(),
            P("seq", None),
            P("seq", None),
            P(),
            P(),
            P(),
            P(),
            P(),
            P(),
            P("seq", None),
        ),
        check_vma=False,
    )
```

profile of v0, /device:TPU:1, one launch (start us, length us, event | category | flops | bytes accessed | tf_op | source)
XLA Modules:
  0.0 970.1 jit_solution(4543117085171972159)
XLA Ops:
  8.7 21.1 %all-gather.2 = bf16[16,96,48]{1,2,0:T(8,128)(2,1)S(1)} all-gather(bf16[1,96,48]{1,2,0:T(8,128)(2,1)} %bitcast.126), channel_id=1, replica_groups=mesh['rep'=8,'seq'=16] {'seq'}, dimensions={0}, use_global_device_ids=true | all-gather | bytes 156672 | tf_op jit(solution)/shard_map/all_gather | solution.py:166
  32.2 107.9 %all-gather.9.cloned.1.call-done = bf16[1536,6400]{1,0:T(8,128)(2,1)} async-done(((bf16[96,6400]{1,0:T(8,128)(2,1)}), bf16[1536,6400]{1,0:T(8,128)(2,1)}) %all-gather.9.cloned.1.call-update) | async-done | bytes 19660816 | tf_op jit(solution)/shard_map/all_gather | solution.py:165
  140.1 11.1 %fusion.119 = (bf16[128,6400]{1,0:T(8,128)(2,1)S(1)}, f32[128,6400]{1,0:T(8,128)}) fusion(bf16[1536,6400]{1,0:T(8,128)(2,1)} %all-gather.9.cloned.1.call-done, bf16[128,1536]{1,0:T(8,128)(2,1)S(1)} %copy-done.6, f32[1536]{0:T(1024)S(1)} %copy-done.30, f32[128]{0:T(128)S(1)} %fusion.100), kind=kOutput, calls=%fused_computation.187 | convolution fusion | flops 2518188032 | bytes 24975872 | tf_op jit(solution)/shard_map/dot_general | solution.py:172
  166.1 19.6 %all-gather.3 = bf16[16,1,48]{2,1,0:T(2,128)(2,1)S(1)} all-gather(bf16[1,1,48]{2,1,0:T(2,128)(2,1)S(1)} %convert_bitcast_fusion), channel_id=1, replica_groups=mesh['rep'=8,'seq'=16] {'seq'}, dimensions={0}, use_global_device_ids=true | all-gather | bytes 1632 | tf_op jit(solution)/shard_map/all_gather | solution.py:19
  191.5 65.8 %all-gather.13.cloned.1.call-done = bf16[768,64,128]{2,1,0:T(8,128)(2,1)} async-done(((bf16[48,64,128]{2,1,0:T(8,128)(2,1)}), bf16[768,64,128]{2,1,0:T(8,128)(2,1)}) %all-gather.13.cloned.1.call-update) | async-done | bytes 12582928 | tf_op jit(solution)/shard_map/all_gather | solution.py:19
  257.4 25.7 %while.24 = (s32[]{:T(128)}, f32[48,64,128]{2,1,0:T(8,128)S(1)}, s32[]{:T(128)}, bf16[16,48]{1,0:T(8,128)(2,1)S(1)}, bf16[16,48,64,128]{3,2,1,0:T(8,128)(2,1)}, /*index=5*/s32[]{:T(128)}, s32[]{:T(128)}) while((s32[]{:T(128)}, f32[48,64,128]{2,1,0:T(8,128)S(1)}, s32[]{:T(128)}, bf16[16,48]{1,0:T(8,128)(2,1)S(1)}, ...), condition=%wide.region_3.4_spmd.clone, body=%wide.region_2.3_spmd.clone.sunk | while | flops 1966132 | bytes 3932753 | solution.py:36
  285.5 8.6 fusion.21
  301.8 33.0 %all-gather.11.cloned.1.call-done = bf16[3072,1536]{1,0:T(8,128)(2,1)} async-done(((bf16[192,1536]{1,0:T(8,128)(2,1)}), bf16[3072,1536]{1,0:T(8,128)(2,1)}) %all-gather.11.cloned.1.call-update) | async-done | bytes 9437200 | tf_op jit(solution)/shard_map/all_gather | solution.py:167
  334.8 8.2 multiply_reduce_fusion.5
  343.1 4.8 multiply_reduce_fusion.6
  354.4 7.7 convolution_convert_fusion.1
  369.2 4.9 fusion.48
  374.2 8.6 fusion.13
  382.7 61.3 %all-gather.15.cloned.1.call-done = bf16[768,64,128]{2,1,0:T(8,128)(2,1)} async-done(((bf16[48,64,128]{2,1,0:T(8,128)(2,1)}), bf16[768,64,128]{2,1,0:T(8,128)(2,1)}) %all-gather.15.cloned.1.call-update) | async-done | bytes 12582928 | tf_op jit(solution)/shard_map/all_gather | solution.py:44
  444.2 33.8 %while.23 = (s32[]{:T(128)}, f32[48,64,128]{2,1,0:T(8,128)S(1)}, s32[]{:T(128)}, bf16[16,48]{1,0:T(8,128)(2,1)}, bf16[16,48,64,128]{3,2,1,0:T(8,128)(2,1)}, /*index=5*/s32[]{:T(128)}, s32[]{:T(128)}, s32[]{:T(128)}, s32[]{:T(128)}) while((s32[]{:T(128)}, f32[48,64,128]{2,1,0:T(8,128)S(1)}, s32[]{:T(128)}, bf16[16,48]{1,0:T(8,128)(2,1)}, ...), condition=%wide.region_7.8_spmd, body=%wide.region_6.7_spmd.sunk | while | flops 1179702 | bytes 3932795 | solution.py:61
  480.0 6.5 multiply_reduce_fusion.4
  516.1 9.6 convolution_convert_fusion
  532.9 6.5 fusion.11
  550.5 112.6 %reduce-scatter.6.cloned.1.call-done = bf16[96,6400]{1,0:T(8,128)(2,1)} async-done(((bf16[1536,6400]{1,0:T(8,128)(2,1)}), bf16[96,6400]{1,0:T(8,128)(2,1)}) %reduce-scatter.6.cloned.1.call-update) | async-done | bytes 1228816 | tf_op jit(solution)/shard_map/reduce_scatter | solution.py:259
  663.2 10.7 %fusion.55 = f32[128,1536]{1,0:T(8,128)S(1)} fusion(bf16[1536,6400]{1,0:T(8,128)(2,1)} %all-gather.9.cloned.1.call-done, bf16[128,3328]{1,0:T(8,128)(2,1)S(1)} %copy-done.23, bf16[128,3072]{1,0:T(8,128)(2,1)S(1)} %copy-done.25), kind=kOutput, calls=%fused_computation.97 | convolution fusion | flops 2519859200 | bytes 22085632 | tf_op jit(solution)/shard_map/tc,dc->td/dot_general | solution.py:241
  675.9 61.3 %reduce-scatter.10.cloned.1.call-done = bf16[96,48]{1,0:T(8,128)(2,1)} async-done(((bf16[1536,48]{1,0:T(8,128)(2,1)}), bf16[96,48]{1,0:T(8,128)(2,1)}) %reduce-scatter.10.cloned.1.call-update) | async-done | bytes 9232
  738.0 22.7 %psum.72 = bf16[96,48]{0,1:T(8,128)(2,1)S(1)} all-reduce(bf16[96,48]{0,1:T(8,128)(2,1)S(1)} %copy.132), channel_id=1, replica_groups=mesh['rep'=8,'seq'=16] {'rep'}, use_global_device_ids=true, to_apply=%region_25.26 | all-reduce | flops 4608 | bytes 18432 | tf_op jit(solution)/shard_map/psum | solution.py:271
  761.4 42.4 %all-reduce.17.cloned.1.call-done = (bf16[96,6400]{1,0:T(8,128)(2,1)}, bf16[192,1536]{1,0:T(8,128)(2,1)}) async-done(((bf16[96,6400]{1,0:T(8,128)(2,1)}, bf16[192,1536]{1,0:T(8,128)(2,1)}), (bf16[96,6400]{1,0:T(8,128)(2,1)}, bf16[192,1536]{1,0:T(8,128)(2,1)})) %all-reduce.17.cloned.1.call-update) | async-done | bytes 1818640 | tf_op jit(solution)/shard_map/psum | solution.py:270
  807.8 146.4 %all-reduce.15.cloned.1.call-done = (f32[1536]{0:T(1024)}, f32[4,3328]{1,0:T(4,128)}, f32[3328]{0:T(1024)}, f32[48]{0:T(128)}, f32[48]{0:T(128)}, /*index=5*/f32[48]{0:T(128)}, f32[3072]{0:T(1024)}) async-done(((f32[1536]{0:T(1024)}, f32[4,3328]{1,0:T(4,128)}, f32[3328]{0:T(1024)}, f32[48]{0:T(128)}, f32[48]{0:T(128)}, /*index=5*/f32[48]{0:T(128)}, f32[3072]{0:T(1024)}), (f32[1536]{0:T(1024)}, ...) | async-done | bytes 85584 | tf_op jit(solution)/shard_map/psum | solution.py:246
  (319 shorter events, 172.4 us)
Async XLA Ops:
  7.2 22.9 %copy-start.6 = (bf16[128,1536]{1,0:T(8,128)(2,1)S(1)}, bf16[128,1536]{1,0:T(8,128)(2,1)}, u32[]{:S(2)}) copy-start(bf16[128,1536]{1,0:T(8,128)(2,1)} %param.18) | copy-start | bytes 1179652
  7.2 23.1 %copy-start.67 = (f32[48]{0:T(128)S(1)}, f32[48]{0:T(128)}, u32[]{:S(2)}) copy-start(f32[48]{0:T(128)} %param.24) | copy-start | bytes 580
  7.2 23.1 %copy-start.30 = (f32[1536]{0:T(1024)S(1)}, f32[1536]{0:T(1024)}, u32[]{:S(2)}) copy-start(f32[1536]{0:T(1024)} %param.19) | copy-start | bytes 18436
  7.2 132.9 %all-gather.9.cloned.1.call-start = ((), (), s32[]{:S(2)}) async-start(), calls=%async_computation.3 | async-start | bytes 20889600 | tf_op jit(solution)/shard_map/all_gather | solution.py:165
  7.9 249.4 %all-gather.13.cloned.1.call-start = ((), (), s32[]{:S(2)}) async-start(), calls=%async_computation.7 | async-start | bytes 13369344 | tf_op jit(solution)/shard_map/all_gather | solution.py:19
  8.7 23.5 %copy-start.63 = (f32[48]{0:T(128)}, f32[48]{0:T(128)S(1)}, u32[]{:S(2)}) copy-start(f32[48]{0:T(128)S(1)} %exp.175) | copy-start | bytes 580
  32.2 122.1 %copy-start.52 = (f32[4,3328]{1,0:T(4,128)S(1)}, f32[4,3328]{1,0:T(4,128)}, u32[]{:S(2)}) copy-start(f32[4,3328]{1,0:T(4,128)} %param.22) | copy-start | bytes 159748
  151.2 4.1 collective-permute-start
  164.6 170.2 %all-gather.11.cloned.1.call-start = ((), (), s32[]{:S(2)}) async-start(), calls=%async_computation.4 | async-start | bytes 10027008 | tf_op jit(solution)/shard_map/all_gather | solution.py:167
  165.3 278.7 %all-gather.15.cloned.1.call-start = ((), (), s32[]{:S(2)}) async-start(), calls=%async_computation.8 | async-start | bytes 13369344 | tf_op jit(solution)/shard_map/all_gather | solution.py:44
  283.0 86.2 %copy-start = (f32[48,64,128]{2,1,0:T(8,128)}, f32[48,64,128]{2,1,0:T(8,128)S(1)}, u32[]{:S(2)}) copy-start(f32[48,64,128]{2,1,0:T(8,128)S(1)} %get-tuple-element.533) | copy-start | bytes 4718596
  297.2 37.6 %copy-start.26 = (f32[3072]{0:T(1024)S(1)}, f32[3072]{0:T(1024)}, u32[]{:S(2)}) copy-start(f32[3072]{0:T(1024)} %param.27) | copy-start | bytes 36868
  354.1 196.3 %reduce-scatter.8.cloned.1.call-start = ((), (), s32[]{:S(2)}) async-start(), calls=%async_computation.6 | async-start | bytes 10027008 | tf_op jit(solution)/shard_map/reduce_scatter | solution.py:265
  362.1 300.9 %reduce-scatter.6.cloned.1.call-start = ((), (), s32[]{:S(2)}) async-start(), calls=%async_computation.5 | async-start | bytes 20889600 | tf_op jit(solution)/shard_map/reduce_scatter | solution.py:259
  510.3 4.7 collective-permute-start.1
  525.7 211.5 %reduce-scatter.10.cloned.1.call-start = ((), (), s32[]{:S(2)}) async-start(), calls=%async_computation.9 | async-start | bytes 417792
  540.0 9.9 %copy-start.68 = (f32[48]{0:T(128)S(1)}, f32[48]{0:T(128)}, u32[]{:S(2)}) copy-start(f32[48]{0:T(128)} %param.25) | copy-start | bytes 580
  548.3 114.9 %copy-start.23 = (bf16[128,3328]{1,0:T(8,128)(2,1)S(1)}, bf16[128,3328]{1,0:T(8,128)(2,1)}, u32[]{:S(2)}) copy-start(bf16[128,3328]{1,0:T(8,128)(2,1)} %copy-done.22) | copy-start | bytes 2555908
  548.3 114.9 %copy-start.25 = (bf16[128,3072]{1,0:T(8,128)(2,1)S(1)}, bf16[128,3072]{1,0:T(8,128)(2,1)}, u32[]{:S(2)}) copy-start(bf16[128,3072]{1,0:T(8,128)(2,1)} %get-tuple-element.613) | copy-start | bytes 2359300
  549.2 254.5 %all-reduce.17.cloned.1.call-start = ((), (), s32[]{:S(2)}) async-start(), calls=%async_computation.11 | async-start | bytes 3637248 | tf_op jit(solution)/shard_map/psum | solution.py:270
  663.1 10.8 %copy-start.8 = (bf16[128,1536]{1,0:T(8,128)(2,1)S(1)}, bf16[128,1536]{1,0:T(8,128)(2,1)}, u32[]{:S(2)}) copy-start(bf16[128,1536]{1,0:T(8,128)(2,1)} %param.18) | copy-start | bytes 1179652
  663.1 10.8 %copy-start.29 = (bf16[1536,48]{0,1:T(8,128)(2,1)S(1)}, bf16[1536,48]{0,1:T(8,128)(2,1)}, u32[]{:S(2)}) copy-start(bf16[1536,48]{0,1:T(8,128)(2,1)} %copy-done.28) | copy-start | bytes 442372
  663.1 10.8 %copy-start.32 = (f32[1536]{0:T(1024)S(1)}, f32[1536]{0:T(1024)}, u32[]{:S(2)}) copy-start(f32[1536]{0:T(1024)} %param.19) | copy-start | bytes 18436
  663.1 291.2 %all-reduce.15.cloned.1.call-start = ((), (), s32[]{:S(2)}) async-start(), calls=%async_computation.10 | async-start | bytes 183296 | tf_op jit(solution)/shard_map/psum | solution.py:246
  (56 other events, 218.5 us)
Sparse Core Ops, SparseCore 0:
  10.2 129.8 all-gather.8
  164.7 92.6 all-gather.12
  259.5 75.2 all-gather.10
  354.3 89.7 all-gather.14
  447.3 86.4 reduce-scatter.7
  537.6 125.3 reduce-scatter.5
  666.8 70.3 reduce-scatter.9
  739.9 63.7 all-reduce.16
  812.0 142.2 all-reduce.14
where the time goes:
time: 979 us; the launch traced here: 970 us
  waiting for transfers between devices  636 us (65%)
  matrix products  108 us (11%)
  other arithmetic  96.8 us (10%)
  blocking collectives  63.5 us (6%)
  local copies, waits for them, and re-layouts  43.9 us (4%)
  between operations  15.3 us (2%)
    psum x1, waiting for transfers between devices, local(): lax.psum((grad_norm_gain, grad_conv_weight, grad_conv_bias, grad_dt_bias,...  146 us
    reduce_scatter x1, waiting for transfers between devices, local(): lax.psum_scatter(grad_main_local.astype(jnp.bfloat16), 'seq', scatter_dim...  113 us
    all_gather x1, waiting for transfers between devices, local(): lax.all_gather(w_main, 'seq', axis=0, tiled=True)  108 us
    all_gather x1, waiting for transfers between devices, carried_in(): lax.all_gather(part.astype(kind), axis)  65.8 us
    unnamed x10, waiting for transfers between devices  62.8 us
    all_gather x1, waiting for transfers between devices, entering_2(): lax.all_gather(a.astype(kind), axis)  61.3 us
    psum x1, waiting for transfers between devices, local(): lax.psum(shards[0].astype(jnp.bfloat16), 'rep').astype(jnp.float32)  42.4 us
    all_gather x1, waiting for transfers between devices, local(): lax.all_gather(w_out, 'seq', axis=0, tiled=True)  33 us
  transfers between devices with their start and end apart: 11, of which 10 were waited for; matrix products, arithmetic and copies ran while one was open for 20% of the time, Pallas kernels for 0%

commit v1 on v0

v1 whole, which is shorter than its diff:
```python
import functools

import jax
import jax.numpy as jnp
from jax import lax
from jax.experimental import pallas as pl
from jax.experimental.pallas import tpu as pltpu
from jax.sharding import Mesh, PartitionSpec as P

EPS = 1e-05
BF = jnp.bfloat16
F32 = jnp.float32
HIGH = lax.Precision.HIGHEST
NX = 4
NZ = 4
D = 1536
HL = 12
PW = 64
HW = 768
NS = 128
L = 128
NC = 4
T = 512
RIM = 16
TR = T + RIM
CC = 1024
CA = 1152
DI = 3072
VMEM = 58 * 1024 * 1024


def call(body, outs, ins, scratch=(), flops=0, smem=1):
    specs = [pl.BlockSpec(memory_space=pltpu.SMEM)] * smem
    specs += [pl.BlockSpec(memory_space=pltpu.VMEM)] * (len(ins) - smem)
    return pl.pallas_call(
        body,
        out_shape=[jax.ShapeDtypeStruct(shape, kind) for shape, kind in outs],
        in_specs=specs,
        out_specs=[pl.BlockSpec(memory_space=pltpu.VMEM)] * len(outs),
        scratch_shapes=[pltpu.VMEM(shape, kind) for shape, kind in scratch],
        compiler_params=pltpu.CompilerParams(vmem_limit_bytes=VMEM),
        cost_estimate=pl.CostEstimate(flops=flops, bytes_accessed=4 << 20, transcendentals=0),
        name=body.__name__,
    )(*ins)


def mm(a, b):
    return lax.dot_general(a, b, (((1,), (0,)), ((), ())), preferred_element_type=F32)


def mm_nt(a, b):
    return lax.dot_general(a, b, (((1,), (1,)), ((), ())), preferred_element_type=F32)


def mm_tn(a, b):
    return lax.dot_general(a, b, (((0,), (0,)), ((), ())), preferred_element_type=F32)


def mm_high(a, b):
    return lax.dot_general(
        a, b, (((1,), (0,)), ((), ())), precision=HIGH, preferred_element_type=F32
    )


def iota2(shape, dim):
    return lax.broadcasted_iota(jnp.int32, shape, dim)


def spread_matrix(kind):
    return (
        lax.shift_right_logical(iota2((128, HW), 1), 6) == iota2((128, HW), 0)
    ).astype(kind)


def spread(v, e):
    hi = v.astype(BF)
    rest = v - hi.astype(F32)
    mid = rest.astype(BF)
    lo = (rest - mid.astype(F32)).astype(BF)
    return mm(hi, e) + mm(mid, e) + mm(lo, e)


def head_sums(v, e):
    hi = v.astype(BF)
    lo = (v - hi.astype(F32)).astype(BF)
    return mm_nt(hi, e) + mm_nt(lo, e)


def sigmoid(v):
    return 1.0 / (1.0 + jnp.exp(-v))


def chunk(ref, c, lanes=slice(None), base=0):
    return ref[pl.ds(pl.multiple_of(base + c * L, 16), L), lanes]


def pack_weights(idx, wm, wd, *rest):
    outs_a, outs_g, sa, sg = rest[:4], rest[4:8], rest[8], rest[9]
    x, core = idx[0], idx[2]
    rows = pl.ds(pl.multiple_of(core * 48, 16), 48)
    for xp in range(NX):
        for zp in range(NZ):
            at = 768 * zp + 192 * xp
            sg[xp, :, 192 * zp : 192 * zp + 192] = wm[rows, at : at + 192]
            sa[xp, :, 192 * zp : 192 * zp + 192] = wm[rows, DI + at : DI + at + 192]
        sa[xp, :, HW:CC] = wm[rows, 2 * DI : 2 * DI + 256]
        sa[xp, :, CC:CA] = wd[xp, rows]
    for k in range(NX):
        to = lax.rem(x + k, NX)
        outs_a[k][...] = sa[to]
        outs_g[k][...] = sg[to]


def norm_rows(idx, t0, t1, t2, t3, gain, normed, tail):
    x = idx[0]
    for k, piece in enumerate((t0, t1, t2, t3)):
        v = piece[...].astype(F32)
        root = lax.rsqrt(jnp.mean(v * v, axis=1, keepdims=True) + EPS)
        at = pl.multiple_of(lax.rem(x + NX - k, NX) * 128, 128)
        normed[pl.ds(at, 128), :] = (v * root * gain[...]).astype(BF)
    tail[...] = normed[T - RIM : T, :]


def turn(idx, normed, rim, nfull, mine, other, scr):
    core = idx[2]
    nfull[0:T, :] = normed[...]
    nfull[T:TR, :] = rim[...]
    blank = jnp.zeros((128 - RIM, 128), F32)
    for j in range(D // 128):
        lanes = slice(128 * j, 128 * j + 128)
        scr[lanes, 0:T] = normed[:, lanes].astype(F32).T.astype(BF)
        edge = jnp.concatenate([rim[:, lanes].astype(F32), blank], axis=0)
        scr[lanes, T : T + 128] = edge.T.astype(BF)
    for block in range(16):
        for out, half in ((mine, core), (other, 1 - core)):
            at = pl.multiple_of(96 * block + 48 * half, 16)
            out[48 * block : 48 * block + 48, :] = scr[pl.ds(at, 48), 0:TR]


def project(idx, nfull, mine, other, par, hp, wa, ci, act, dsl, sm, sc, fp, scr):
    x, z, core = idx[0], idx[1], idx[2]
    for step in range(NZ):
        for k in range(NX):
            block = 4 * lax.rem(z + NZ - step, NZ) + lax.rem(x + NX - k, NX)
            for ref, half in ((mine, core), (other, 1 - core)):
                at = pl.multiple_of(96 * block + 48 * half, 16)
                row = 192 * step + 48 * k
                wa[pl.ds(at, 48), :] = ref[row : row + 48, :]

    raw = mm(nfull[0:T, :], wa[:, CC:CA]) + hp[0:1, :]
    held = iota2((T, 128), 1) < HL
    dt = jnp.where(held, jnp.maximum(raw, 0.0) + jnp.log1p(jnp.exp(-jnp.abs(raw))), 0.0)
    sm[0] = dt
    sm[2] = sigmoid(raw)
    decay = -dt * jnp.exp(hp[1:2, :])
    tri = (iota2((L, L), 0) >= iota2((L, L), 1)).astype(F32)
    for c in range(NC):
        sm[1, c * L : c * L + L, :] = mm_high(tri, decay[c * L : c * L + L])

    @pl.loop(0, 4)
    def _(j):
        lanes = pl.ds(pl.multiple_of(j * 256, 256), 256)
        low = mm(nfull[...], wa[:, lanes]).astype(BF)
        ci[:, lanes] = low
        scr[RIM:TR, :] = low[0:T].astype(F32)
        scr[0:RIM, :] = low[T:TR].astype(F32)
        pre = par[4:5, lanes] + par[0:1, lanes] * scr[13 : 13 + T, :]
        for k in range(1, 4):
            pre = pre + par[k : k + 1, lanes] * scr[13 + k : 13 + k + T, :]
        s = sigmoid(pre)
        act[:, lanes] = (pre * s).astype(BF)
        dsl[:, lanes] = (s * (1.0 + pre * (1.0 - s))).astype(BF)

    e = spread_matrix(BF)
    final = jnp.zeros((NS, HW), F32)
    total = jnp.zeros((8, HW), F32)
    for c in range(NC):
        rows = slice(c * L, c * L + L)
        s = sm[1, rows, :]
        last = s[L - 1 : L, :]
        w = spread(jnp.exp(last - s) * sm[0, rows, :], e)
        vw = (act[rows, 0:HW].astype(F32) * w).astype(BF)
        part = mm_tn(act[rows, HW : HW + NS], vw)
        sc[c] = part
        last_e = spread(jnp.broadcast_to(last, (8, 128)), e)
        final = jnp.exp(last_e[0:1]) * final + part
        total = total + last_e
    pack_state(fp, final, total)


def pack_state(fp, state, total):
    hi = total.astype(BF)
    lo = (total - hi.astype(F32)).astype(BF)
    fp[0:NS, :] = state.astype(BF)
    fp[NS : NS + 16, :] = jnp.concatenate(
        [hi.astype(F32), lo.astype(F32)], axis=0
    ).astype(BF)


def incoming(p1, p2, p3):
    t1 = p1[NS : NS + 16, :].astype(F32)
    t2 = p2[NS : NS + 16, :].astype(F32)
    t1 = t1[0:1] + t1[8:9]
    t2 = t2[0:1] + t2[8:9]
    return (
        p1[0:NS, :].astype(F32)
        + jnp.exp(t1) * p2[0:NS, :].astype(F32)
        + jnp.exp(t1 + t2) * p3[0:NS, :].astype(F32)
    )


def gates(idx, nfull, mine, other, cot, gate, gny, wg, wo):
    x, z, core = idx[0], idx[1], idx[2]
    for step in range(NZ):
        to = lax.rem(z + NZ - step, NZ)
        for ref, half in ((mine, core), (other, 1 - core)):
            at = pl.multiple_of(192 * to + 96 * half, 16)
            wo[pl.ds(at, 96), :] = ref[192 * step : 192 * step + 96, :]
            for k in range(NX):
                block = 4 * to + lax.rem(x + NX - k, NX)
                at = pl.multiple_of(96 * block + 48 * half, 16)
                row = 192 * step + 96 + 48 * (k // 2)
                lane = HW * (k % 2)
                wg[pl.ds(at, 48), :] = ref[row : row + 48, lane : lane + HW]

    @pl.loop(0, 3)
    def _(j):
        lanes = pl.ds(pl.multiple_of(j * 256, 256), 256)
        gate[:, lanes] = mm(nfull[0:T, :], wg[:, lanes])
        gny[:, lanes] = mm_nt(cot[...], wo[lanes, :])


def within(idx, act, sm, hp, yi):
    e = spread_matrix(BF)
    skip = spread(jnp.broadcast_to(hp[2:3, :], (8, 128)), e)[0:1]
    left = iota2((L, 128), 1) < PW
    causal = iota2((L, L), 0) >= iota2((L, L), 1)

    @pl.loop(0, NC)
    def _(c):
        rows = pl.ds(pl.multiple_of(c * L, L), L)
        s = sm[1, rows, :]
        s_t = s.T
        v = act[rows, 0:HW].astype(F32)
        u = v * spread(sm[0, rows, :], e)
        scores = mm_nt(act[rows, HW + NS : CC], act[rows, HW : HW + NS])
        for j in range(HL // 2):
            parts = []
            for h in (2 * j, 2 * j + 1):
                gap = s[:, h : h + 1] - s_t[h : h + 1, :]
                parts.append((scores * jnp.exp(jnp.where(causal, gap, -1e30))).astype(BF))
            pair = u[:, 128 * j : 128 * j + 128]
            both = jnp.concatenate(
                [jnp.where(left, pair, 0.0), jnp.where(left, 0.0, pair)], axis=0
            ).astype(BF)
            yi[rows, 128 * j : 128 * j + 128] = mm(jnp.concatenate(parts, axis=1), both)
        yi[rows, :] += skip * v


def mix(idx, yi, act, sm, sc, p1, p2, p3, gate, gny, par, mixed, hin, sums):
    e = spread_matrix(BF)
    ones = jnp.ones((8, HW), BF)

    def rowsum(v):
        hi = v.astype(BF)
        lo = (v - hi.astype(F32)).astype(BF)
        return mm_nt(ones, hi) + mm_nt(ones, lo)

    state = incoming(p1, p2, p3)
    for c in range(NC):
        rows = slice(c * L, c * L + L)
        s = sm[1, rows, :]
        low = state.astype(BF)
        hin[c] = low
        y = yi[rows, :] + spread(jnp.exp(s), e) * mm(act[rows, HW + NS : CC], low)
        mixed[rows, :] = y
        z = gate[rows, :]
        g = y * (z * sigmoid(z))
        sq = rowsum(g * g)
        sg = rowsum(g * (gny[rows, :] * par[5:6, 0:HW]))
        sums[:, rows] = jnp.where(iota2((8, L), 0) == 0, sq, sg)
        last = spread(jnp.broadcast_to(s[L - 1 : L, :], (8, 128)), e)[0:1]
        state = jnp.exp(last) * state + sc[c]


def gated(
    idx, mixed, gate, gny, act, sm, s0, s1, s2, s3, wo, par,
    ny, gmix, ggate, bo, rp, small,
):
    e = spread_matrix(BF)
    sums = s0[...] + s1[...] + s2[...] + s3[...]
    gain = par[5:6, 0:HW]
    pick0 = (iota2((8, 128), 0) == 0).astype(F32)
    pick1 = (iota2((8, 128), 0) == 1).astype(F32)
    grad_gain = jnp.zeros((1, HW), F32)
    grad_skip = jnp.zeros((1, HW), F32)
    pulls = []
    totals = []
    for c in range(NC):
        rows = slice(c * L, c * L + L)
        here = sums[:, rows]
        sq = lax.dot_general(
            here, pick0, (((0,), (0,)), ((), ())), precision=HIGH, preferred_element_type=F32
        )
        sg = lax.dot_general(
            here, pick1, (((0,), (0,)), ((), ())), precision=HIGH, preferred_element_type=F32
        )
        r1 = lax.rsqrt(sq * (1.0 / DI) + EPS)
        pull = r1 * r1 * (sg * (1.0 / DI))
        r1 = jnp.concatenate([r1] * 6, axis=1)
        pull = jnp.concatenate([pull] * 6, axis=1)
        y = mixed[rows, :]
        z = gate[rows, :]
        sz = sigmoid(z)
        sil = z * sz
        g = y * sil
        gn = gny[rows, :]
        ghat = g * r1
        ny[rows, :] = (ghat * gain).astype(BF)
        grad_gain = grad_gain + jnp.sum(gn * ghat, axis=0, keepdims=True)
        gg = r1 * (gn * gain - g * pull)
        gm = gg * sil
        gmix[rows, :] = gm.astype(BF)
        ggate[rows, :] = (gg * y * (sz * (1.0 + z * (1.0 - sz)))).astype(BF)
        grad_skip = grad_skip + jnp.sum(gm * act[rows, 0:HW].astype(F32), axis=0, keepdims=True)
        s = sm[1, rows, :]
        pulls.append(mm_tn(act[rows, HW + NS : CC], (gm * spread(jnp.exp(s), e)).astype(BF)))
        totals.append(spread(jnp.broadcast_to(s[L - 1 : L, :], (8, 128)), e))
    state = jnp.zeros((NS, HW), F32)
    total = jnp.zeros((8, HW), F32)
    for c in reversed(range(NC)):
        state = jnp.exp(totals[c][0:1]) * state + pulls[c]
        total = total + totals[c]
    pack_state(rp, state, total)
    small[0:1, :] = grad_gain
    small[1:2, :] = grad_skip

    @pl.loop(0, 6)
    def _(j):
        lanes = pl.ds(pl.multiple_of(j * 256, 256), 256)
        bo[:, lanes] = mm(ny[...], wo[:, lanes]).astype(BF)


def within_back(idx, act, gmix, sm, gu, gbc, dsi, rw):
    left = iota2((L, 128), 1) < PW
    lane = iota2((L, 128), 1)
    causal = iota2((L, L), 1) >= iota2((L, L), 0)
    rw[...] = jnp.zeros_like(rw)

    @pl.loop(0, NC)
    def _(c):
        rows = pl.ds(pl.multiple_of(c * L, L), L)
        s = sm[1, rows, :]
        s_t = s.T
        dt = sm[0, rows, :]
        b = act[rows, HW : HW + NS]
        r = act[rows, HW + NS : CC]
        scores = mm_nt(b, r)
        grad_scores = jnp.zeros((L, L), F32)
        cols = jnp.zeros((L, 128), F32)
        for j in range(HL // 2):
            v = act[rows, 128 * j : 128 * j + 128].astype(F32)
            g = gmix[rows, 128 * j : 128 * j + 128]
            gf = g.astype(F32)
            parts = []
            for i in range(2):
                h = 2 * j + i
                gap = s_t[h : h + 1, :] - s[:, h : h + 1]
                q = jnp.exp(jnp.where(causal, gap, -1e30))
                own = jnp.where(left, v, 0.0) if i == 0 else jnp.where(left, 0.0, v)
                vg = mm_nt(own.astype(BF), g) * (q * dt[:, h : h + 1])
                grad_scores = grad_scores + vg
                w = scores * vg
                rw[h : h + 1, :] = jnp.sum(w, axis=0, keepdims=True)
                cols = jnp.where(lane == h, jnp.sum(w, axis=1, keepdims=True), cols)
                parts.append((scores * q).astype(BF))
            both = jnp.concatenate(
                [jnp.where(left, gf, 0.0), jnp.where(left, 0.0, gf)], axis=0
            ).astype(BF)
            gu[rows, 128 * j : 128 * j + 128] = mm(jnp.concatenate(parts, axis=1), both)
        dsi[rows, :] = rw[...].T - cols
        low = grad_scores.astype(BF)
        gbc[rows, 0:NS] = mm(low, r)
        gbc[rows, NS : 2 * NS] = mm_tn(low, b)


def across_back(
    idx, act, gmix, sm, gu, gbc, dsi, hin, p1, p2, p3, dsl, ci, par, hp,
    gpa, small, hsm, gps, cis,
):
    e = spread_matrix(BF)
    skip = spread(jnp.broadcast_to(hp[2:3, :], (8, 128)), e)[0:1]
    rate = jnp.exp(hp[1:2, :])
    upper = (iota2((L, L), 1) >= iota2((L, L), 0)).astype(F32)
    below = (iota2((L, L), 0) > iota2((L, L), 1)).astype(F32)
    gps[0:RIM, :] = jnp.zeros((RIM, CC), F32)
    gps[RIM + T : RIM + T + 16, :] = jnp.zeros((16, CC), F32)
    state = incoming(p1, p2, p3)
    grad_log = jnp.zeros((1, 128), F32)
    grad_bias = jnp.zeros((1, 128), F32)
    gpa[T:TR, CC:CA] = jnp.zeros((RIM, 128), BF)
    for c in reversed(range(NC)):
        rows = slice(c * L, c * L + L)
        b = act[rows, HW : HW + NS]
        r = act[rows, HW + NS : CC]
        low = state.astype(BF)
        s = sm[1, rows, :]
        dt = sm[0, rows, :]
        last = s[L - 1 : L, :]
        tail_e = spread(jnp.exp(last - s), e)
        dt_e = spread(dt, e)
        grow_e = spread(jnp.exp(s), e)
        last_e = jnp.exp(spread(jnp.broadcast_to(last, (8, 128)), e)[0:1])
        v = act[rows, 0:HW].astype(F32)
        g = gmix[rows, :].astype(F32)
        carried = tail_e * mm(b, low)
        grad_u = gu[rows, :] + carried
        u = v * dt_e
        grad_v = dt_e * grad_u + skip * g
        grad_b = gbc[rows, 0:NS] + mm_nt((u * tail_e).astype(BF), low)
        gs = (g * grow_e).astype(BF)
        h = hin[c]
        grad_c = gbc[rows, NS : 2 * NS] + mm_nt(gs, h)
        inter = head_sums(g * (grow_e * mm(r, h)), e)
        kept = head_sums(u * carried, e)
        grad_step = head_sums(v * grad_u, e)
        cross = jnp.sum(h.astype(F32) * state, axis=0, keepdims=True) * last_e
        cross = head_sums(jnp.broadcast_to(cross, (8, HW)), e)[0:1]
        grad_a = mm_high(upper, dsi[rows, :] + inter) + mm_high(below, kept) + cross
        grad_raw = (grad_step - rate * grad_a) * sm[2, rows, :]
        grad_log = grad_log + jnp.sum(grad_a * dt, axis=0, keepdims=True)
        grad_bias = grad_bias + jnp.sum(grad_raw, axis=0, keepdims=True)
        held = iota2((L, 128), 1) < HL
        gpa[rows, CC:CA] = jnp.where(held, grad_raw, 0.0).astype(BF)
        d = dsl[rows, :].astype(F32)
        to = slice(RIM + c * L, RIM + c * L + L)
        gps[to, 0:HW] = grad_v * d[:, 0:HW]
        gps[to, HW : HW + NS] = grad_b * d[:, HW : HW + NS]
        gps[to, HW + NS : CC] = grad_c * d[:, HW + NS : CC]
        state = last_e * state + mm_tn(r, gs)
    hsm[0:1, :] = grad_bias
    hsm[1:2, :] = -rate * grad_log

    @pl.loop(0, 4)
    def _(j):
        lanes = pl.ds(pl.multiple_of(j * 256, 256), 256)
        cis[RIM:TR, :] = ci[0:T, lanes].astype(F32)
        cis[0:RIM, :] = ci[T:TR, lanes].astype(F32)
        gp = gps[RIM : RIM + T, lanes]
        small[4:5, lanes] = jnp.sum(gp, axis=0, keepdims=True)
        out = par[3:4, lanes] * gps[0:TR, lanes]
        for k in range(4):
            small[k : k + 1, lanes] = jnp.sum(
                gp * cis[13 + k : 13 + k + T, :], axis=0, keepdims=True
            )
            if k < 3:
                out = out + par[k : k + 1, lanes] * gps[3 - k : 3 - k + TR, lanes]
        low = out.astype(BF)
        gpa[0:T, lanes] = low[RIM:TR]
        gpa[T:TR, lanes] = low[0:RIM]


def rim_back(idx, gpa, wa, out):
    out[...] = mm_nt(gpa[T:TR, :], wa[...]).astype(BF)


def normed_back(idx, gpa, ggate, wa, wg, nfull, rim, gain, o0, o1, o2, o3, gsum, acc):
    x = idx[0]

    @pl.loop(0, 6)
    def _(j):
        lanes = pl.ds(pl.multiple_of(j * 256, 256), 256)
        acc[:, lanes] = mm_nt(gpa[0:T, :], wa[lanes, :]) + mm_nt(ggate[...], wg[lanes, :])

    acc[T - RIM : T, :] += rim[...].astype(F32)
    gsum[...] = jnp.broadcast_to(
        jnp.sum(acc[...] * nfull[0:T, :].astype(F32), axis=0, keepdims=True) / gain[...],
        (8, D),
    )
    for k, out in enumerate((o0, o1, o2, o3)):
        at = pl.multiple_of(lax.rem(x + k, NX) * 128, 128)
        out[...] = acc[pl.ds(at, 128), :].astype(out.dtype)


def finish_out(idx, tokens, summed, out):
    out[...] = (tokens[...].astype(F32) + summed[...].astype(F32)).astype(BF)


def finish_back(idx, tokens, cot, g0, g1, g2, g3, gain, out):
    v = tokens[...].astype(F32)
    root = lax.rsqrt(jnp.mean(v * v, axis=1, keepdims=True) + EPS)
    q = (
        g0[...] + g1[...].astype(F32) + g2[...].astype(F32) + g3[...].astype(F32)
    ) * gain[...]
    pull = jnp.mean(q * v, axis=1, keepdims=True)
    out[...] = (cot[...].astype(F32) + root * (q - v * (root * root) * pull)).astype(BF)


def grad_early(idx, ny, cot, ggate, turned, half, out, nyt, rows):
    which = lax.rem(idx[2] + half, 2)
    for j in range(HW // 128):
        lanes = slice(128 * j, 128 * j + 128)
        nyt[lanes, :] = ny[:, lanes].astype(F32).T.astype(BF)
    for z in range(NZ):
        at = pl.multiple_of(192 * z + 96 * which, 16)
        rows[96 * z : 96 * z + 96, :] = nyt[pl.ds(at, 96), :]
    @pl.loop(0, 6)
    def _(j):
        lanes = pl.ds(pl.multiple_of(j * 256, 256), 256)
        part = mm(rows[...], cot[:, lanes])
        for z in range(NZ):
            out[192 * z : 192 * z + 96, lanes] = part[96 * z : 96 * z + 96].astype(BF)
    for z in range(NZ):
        part = mm(turned[192 * z : 192 * z + 192, 0:T], ggate[...]).astype(BF)
        for xp in range(NX):
            at = 192 * z + 96 + 48 * (xp // 2)
            lane = HW * (xp % 2)
            out[at : at + 48, lane : lane + HW] = part[48 * xp : 48 * xp + 48]


def early_other(idx, ny, cot, ggate, turned, out, nyt, rows):
    grad_early(idx, ny, cot, ggate, turned, 1, out, nyt, rows)


def early_mine(idx, ny, cot, ggate, turned, got, out, nyt, rows):
    grad_early(idx, ny, cot, ggate, turned, 0, out, nyt, rows)
    out[...] = (out[...].astype(F32) + got[...].astype(F32)).astype(BF)


def late_other(idx, gpa, turned, out):
    for z in range(NZ):
        rows = slice(192 * z, 192 * z + 192)
        out[rows, :] = mm(turned[rows, :], gpa[...]).astype(BF)


def late_mine(idx, gpa, turned, got, out):
    for z in range(NZ):
        rows = slice(192 * z, 192 * z + 192)
        out[rows, :] = (mm(turned[rows, :], gpa[...]) + got[rows, :].astype(F32)).astype(BF)


def small_pack(idx, gsum, conv, gains, heads, out):
    e = spread_matrix(BF)
    for j in range(3):
        out[j : j + 1, :] = gsum[0:1, 512 * j : 512 * j + 512]
    for k in range(5):
        for j in range(2):
            out[3 + 2 * k + j : 4 + 2 * k + j, :] = conv[k : k + 1, 512 * j : 512 * j + 512]
    out[13:14, :] = gains[0:1, 0:512]
    out[14:15, 0:256] = gains[0:1, 512:768]
    skip = head_sums(jnp.broadcast_to(gains[1:2, :], (8, HW)), e)[0:1]
    out[14:15, 256:384] = skip
    out[14:15, 384:512] = heads[0:1, :]
    out[15:16, 0:128] = heads[1:2, :]
    out[15:16, 128:512] = jnp.zeros((1, 384), F32)


def small_add(idx, a, b, out):
    out[...] = a[...] + b[...]


def halves(v):
    hi = v.astype(BF).astype(F32)
    return jnp.concatenate([hi, v - hi], axis=0).astype(BF)


def joined(v):
    v = v.astype(F32)
    return v[0:16] + v[16:32]


def split_y(idx, late, early, a, b, c, d, o0, o1, o2, o3, scr):
    y = idx[3]
    small = halves(a[...] + b[...] + c[...] + d[...])
    for q in range(4):
        at = 192 * q
        scr[q, 0:192, 0:192] = late[:, at : at + 192]
        scr[q, 0:192, 192:256] = late[:, HW + 64 * q : HW + 64 * q + 64]
        scr[q, 0:192, 448:512] = late[:, CC : CC + 64]
        for xp in range(NX):
            row = 96 + 48 * (xp // 2)
            lane = HW * (xp % 2) + at
            scr[q, 48 * xp : 48 * xp + 48, 256:448] = early[row : row + 48, lane : lane + 192]
        scr[q, 192:288, 0:384] = early[0:96, 384 * q : 384 * q + 384]
        scr[q, 192:288, 384:512] = jnp.zeros((96, 128), BF)
        scr[q, 288:320, :] = small
    for k, out in enumerate((o0, o1, o2, o3)):
        out[...] = scr[lax.rem(y + k, 4)]


def sum_y(idx, a, b, c, d, o0, o1, o2, o3, wo, scr):
    x = idx[0]
    total = a[0:288].astype(F32) + b[0:288].astype(F32)
    total = (total + (c[0:288].astype(F32) + d[0:288].astype(F32))).astype(BF)
    scr[...] = total[0:192]
    wo[...] = total[192:288]
    small = halves(
        joined(a[288:320]) + joined(b[288:320]) + (joined(c[288:320]) + joined(d[288:320]))
    )
    for k, out in enumerate((o0, o1, o2, o3)):
        at = pl.multiple_of(lax.rem(x + k, NX) * 48, 16)
        out[0:48, :] = scr[pl.ds(at, 48), :]
        out[48:80, :] = small


def arrange_x(idx, a, b, c, d, wo, out, gain, conv, ogain, heads, scr):
    x = idx[0]
    shared = jnp.zeros((48, 64), F32)
    for k, ref in enumerate((a, b, c, d)):
        source = lax.rem(x + NX - k, NX)
        out[pl.ds(pl.multiple_of(source * 48, 16), 48), :] = ref[0:48, :]
        shared = shared + ref[0:48, 192:256].astype(F32)
        scr[source] = joined(ref[48:80, :])
    out[0:48, 192:256] = shared.astype(BF)
    out[192:288, :] = wo[...]
    both = scr[0] + scr[1] + (scr[2] + scr[3])
    for j in range(3):
        gain[0:1, 512 * j : 512 * j + 512] = both[j : j + 1, :]
    for k in range(5):
        conv[k : k + 1, DI : DI + 256] = both[4 + 2 * k : 5 + 2 * k, 256:512]
    heads[...] = jnp.zeros_like(heads)
    for xp in range(NX):
        own = scr[xp]
        for q in range(4):
            lane = 768 * q + 192 * xp
            for k in range(5):
                for at, size in pieces(192 * q, 192):
                    conv[k : k + 1, lane + at - 192 * q : lane + at - 192 * q + size] = own[
                        3 + 2 * k + at // 512 : 4 + 2 * k + at // 512, at % 512 : at % 512 + size
                    ]
            for at, size in pieces(192 * q, 192):
                ogain[0:1, lane + at - 192 * q : lane + at - 192 * q + size] = own[
                    13 + at // 512 : 14 + at // 512, at % 512 : at % 512 + size
                ]
            to = slice(12 * q + 3 * xp, 12 * q + 3 * xp + 3)
            heads[0:1, to] = own[14:15, 384 + 3 * q : 387 + 3 * q]
            heads[1:2, to] = own[15:16, 3 * q : 3 * q + 3]
            heads[2:3, to] = own[14:15, 256 + 3 * q : 259 + 3 * q]


def pieces(at, size):
    end = at + size
    while at < end:
        step = min(end, (at // 512 + 1) * 512) - at
        yield at, step
        at += step


def finish_weights(idx, a, b, c, d, other, gmain, gdt, gout, scr):
    y, core = idx[3], idx[2]
    for half in range(2):
        place = lax.rem(core + half, 2)
        for k, ref in enumerate((a, b, c, d)):
            source = lax.rem(y + 4 - k, 4)
            scr[source] = ref[...] if half == 0 else other[288 * k : 288 * k + 288, :]
        rows = pl.ds(pl.multiple_of(48 * place, 16), 48)
        long = pl.ds(pl.multiple_of(96 * place, 16), 96)
        for q in range(4):
            gout[long, 384 * q : 384 * q + 384] = scr[q, 192:288, 0:384].astype(F32)
            gmain[rows, 6144 + 64 * q : 6144 + 64 * q + 64] = scr[q, 0:48, 192:256].astype(F32)
            for xp in range(NX):
                lane = 768 * q + 192 * xp
                part = scr[q, 48 * xp : 48 * xp + 48, :].astype(F32)
                gmain[rows, lane : lane + 192] = part[:, 256:448]
                gmain[rows, DI + lane : DI + lane + 192] = part[:, 0:192]
        for xp in range(NX):
            part = scr[0, 48 * xp : 48 * xp + 48, 448:512].astype(F32)
            for q in range(4):
                gdt[rows, 12 * q + 3 * xp : 12 * q + 3 * xp + 3] = part[:, 3 * q : 3 * q + 3]


def round_shift(v, axis, k, n=4):
    return lax.ppermute(v, axis, [(s, (s + k) % n) for s in range(n)])


def onward(v, k):
    return lax.ppermute(v, "z", [(s, s + k) for s in range(NZ) if 0 <= s + k < NZ])


def around(v, axis, n=4):
    return [v] + [round_shift(v, axis, k, n) for k in range(1, n)]


def after(value, *others):
    return lax.optimization_barrier((value,) + others)[0]


def local(
    tokens, norm_gain, w_main, w_dt, conv_weight, conv_bias, dt_bias, a_log, skip_gain,
    out_gain, w_out, cotangent,
):
    x, z, core, y = (lax.axis_index(name) for name in ("x", "z", "core", "y"))
    idx = jnp.stack([x, z, core, y]).astype(jnp.int32)

    def mine(v):
        shape = v.shape[:-1]
        v = v.reshape(shape + (NZ, NX, v.shape[-1] // 16))
        return lax.dynamic_index_in_dim(v, x, v.ndim - 2, False).reshape(shape + (-1,))

    par = jnp.concatenate(
        [
            jnp.concatenate([mine(conv_weight[:, :DI]), conv_weight[:, DI:]], axis=1),
            jnp.concatenate([mine(conv_bias[:DI]), conv_bias[DI:]])[None],
            jnp.pad(mine(out_gain)[None], ((0, 2), (0, CC - HW))),
        ],
        axis=0,
    )
    hp = jnp.pad(jnp.stack([mine(dt_bias), mine(a_log), mine(skip_gain)]), ((0, 5), (0, 128 - HL)))
    gain = norm_gain[None]

    wd = jnp.pad(
        w_dt.reshape(96, NZ, NX, 3).transpose(2, 0, 1, 3).reshape(NX, 96, HL),
        ((0, 0), (0, 0), (0, 128 - HL)),
    )
    packed = call(
        pack_weights,
        [((48, CA), BF)] * 4 + [((48, HW), BF)] * 4,
        [idx, w_main, wd],
        [((NX, 48, CA), BF), ((NX, 48, HW), BF)],
    )
    wa_x = [packed[0]] + [round_shift(packed[k], "x", k) for k in range(1, 4)]
    wa_z = around(jnp.concatenate(wa_x, axis=0), "z")
    toks = around(after(tokens, wa_x[1], wa_x[2], wa_x[3]), "x")
    wa_mine = jnp.concatenate(wa_z, axis=0)
    wa_other = round_shift(wa_mine, "core", 1, 2)
    late = after(packed[4], *toks[1:])
    wg_x = [late] + [round_shift(packed[4 + k], "x", k) for k in range(1, 4)]
    wo_half = lax.dynamic_slice_in_dim(w_out, core * 96, 96, 0)
    go = jnp.concatenate(
        [
            wo_half,
            jnp.concatenate([wg_x[0], wg_x[1]], axis=1),
            jnp.concatenate([wg_x[2], wg_x[3]], axis=1),
        ],
        axis=0,
    )
    go_mine = jnp.concatenate(around(after(go, *wa_z[1:]), "z"), axis=0)
    go_other = round_shift(go_mine, "core", 1, 2)
    cot = lax.all_gather(after(cotangent, *toks[1:]), "x", axis=0, tiled=True)

    normed, tail = call(
        norm_rows, [((T, D), BF), ((RIM, D), BF)], [idx, *toks, gain], flops=1 << 28
    )
    rim = onward(tail, 1)
    nfull, nt_mine, nt_other = call(
        turn,
        [((TR, D), BF), ((HW, TR), BF), ((HW, TR), BF)],
        [idx, normed, rim],
        [((D, T + 128), BF)],
        flops=1 << 30,
    )
    wa, ci, act, dsl, sm, sc, fp = call(
        project,
        [
            ((D, CA), BF), ((TR, CC), BF), ((T, CC), BF), ((T, CC), BF),
            ((3, T, 128), F32), ((NC, NS, HW), F32), ((NS + 16, HW), BF),
        ],
        [idx, nfull, wa_mine, wa_other, par, hp],
        [((TR, 256), F32)],
        flops=6 << 30,
    )
    states = [onward(fp, k) for k in (1, 2, 3)]
    (yi,) = call(within, [((T, HW), F32)], [idx, act, sm, hp], flops=6 << 30)
    gate, gny, wg, wo = call(
        gates,
        [((T, HW), F32), ((T, HW), F32), ((D, HW), BF), ((HW, D), BF)],
        [idx, nfull, go_mine, go_other, cot],
        flops=6 << 30,
    )
    mixed, hin, sums = call(
        mix,
        [((T, HW), F32), ((NC, NS, HW), BF), ((8, T), F32)],
        [idx, yi, act, sm, sc, *states, gate, gny, par],
        flops=4 << 30,
    )
    ny, gmix, ggate, bo, rp, small_g = call(
        gated,
        [
            ((T, HW), BF), ((T, HW), BF), ((T, HW), BF), ((T, D), BF), ((NS + 16, HW), BF),
            ((8, HW), F32),
        ],
        [idx, mixed, gate, gny, act, sm, *around(sums, "x"), wo, par],
        flops=4 << 30,
    )
    pulls = [onward(rp, -k) for k in (1, 2, 3)]
    gu, gbc, dsi = call(
        within_back,
        [((T, HW), F32), ((T, 2 * NS), F32), ((T, 128), F32)],
        [idx, act, gmix, sm],
        [((128, 128), F32)],
        flops=6 << 30,
    )
    early_scratch = [((HW, T), BF), ((HW // 2, T), BF)]
    (early,) = call(
        early_other, [((HW, D), BF)], [idx, ny, cot, ggate, nt_other], early_scratch, 3 << 30
    )
    got = round_shift(early, "core", 1, 2)
    (early,) = call(
        early_mine, [((HW, D), BF)], [idx, ny, cot, ggate, nt_mine, got], early_scratch, 3 << 30
    )
    early = lax.psum_scatter(early, "z", scatter_dimension=0, tiled=True)
    bo = lax.psum_scatter(bo, "x", scatter_dimension=0, tiled=True)
    gpa, small_c, small_h = call(
        across_back,
        [((TR, CA), BF), ((8, CC), F32), ((8, 128), F32)],
        [idx, act, gmix, sm, gu, gbc, dsi, hin, *pulls, dsl, ci, par, hp],
        [((T + 32, CC), F32), ((TR, 256), F32)],
        flops=8 << 30,
    )
    (late,) = call(late_other, [((HW, CA), BF)], [idx, gpa, nt_other], flops=2 << 30)
    got = round_shift(late, "core", 1, 2)
    (spill,) = call(rim_back, [((RIM, D), BF)], [idx, gpa, wa])
    spill = onward(spill, -1)
    (late,) = call(late_mine, [((HW, CA), BF)], [idx, gpa, nt_mine, got], flops=2 << 30)
    late = lax.psum_scatter(late, "z", scatter_dimension=0, tiled=True)
    gn0, gn1, gn2, gn3, gsum = call(
        normed_back,
        [((128, D), F32), ((128, D), BF), ((128, D), BF), ((128, D), BF), ((8, D), F32)],
        [idx, gpa, ggate, wa, wg, nfull, spill, gain],
        [((T, D), F32)],
        flops=4 << 30,
    )
    gns = [gn0] + [round_shift(b, "x", k) for k, b in ((1, gn1), (2, gn2), (3, gn3))]
    (grad_tokens,) = call(finish_back, [((128, D), BF)], [idx, tokens, cotangent, *gns, gain])
    (block_out,) = call(finish_out, [((128, D), BF)], [idx, tokens, bo])

    (small,) = call(small_pack, [((16, 512), F32)], [idx, gsum, small_c, small_g, small_h])
    (small,) = call(small_add, [((16, 512), F32)], [idx, small, round_shift(small, "core", 1, 2)])
    parts = call(
        split_y,
        [((320, 512), BF)] * 4,
        [idx, late, early, *around(small, "z")],
        [((4, 288 + 32, 512), BF)],
    )
    parts = [parts[0]] + [round_shift(parts[k], "y", k) for k in (1, 2, 3)]
    parts = call(
        sum_y,
        [((80, 512), BF)] * 4 + [((96, 512), BF)],
        [idx, *parts],
        [((192, 512), BF)],
    )
    wo_part = parts[4]
    parts = [parts[0]] + [round_shift(parts[k], "x", k) for k in (1, 2, 3)]
    final, g_gain, g_conv, g_ogain, g_heads = call(
        arrange_x,
        [((288, 512), BF), ((1, D), F32), ((8, DI + 256), F32), ((1, DI), F32), ((8, 128), F32)],
        [idx, *parts, wo_part],
        [((4, 16, 512), F32)],
    )
    finals = around(final, "y")
    other = round_shift(jnp.concatenate(finals, axis=0), "core", 1, 2)
    g_main, g_dt, g_out = call(
        finish_weights,
        [((96, 6400), F32), ((96, 48), F32), ((192, D), F32)],
        [idx, *finals, other],
        [((4, 288, 512), BF)],
    )
    return (
        block_out, grad_tokens, g_gain[0], g_main, g_dt, g_conv[:4], g_conv[4],
        g_heads[0, :48], g_heads[1, :48], g_heads[2, :48], g_ogain[0], g_out,
    )


def solution(mesh):
    grid = Mesh(mesh.devices.reshape(4, 2, 4, 4), ("y", "core", "z", "x"))
    rows = P(("y", "core", "z", "x"), None)
    shard = P(("z", "x"), None)
    whole = P()
    return jax.shard_map(
        local,
        mesh=grid,
        in_specs=(
            rows, whole, shard, shard, whole, whole, whole, whole, whole, whole, shard, rows,
        ),
        out_specs=(
            rows, rows, whole, shard, shard, whole, whole, whole, whole, whole, whole, shard,
        ),
        check_vma=False,
    )
```

time: 979 us -> 392 us (0.40)
  waiting for transfers between devices: 636 us -> 137 us
  Pallas kernels: 0 us -> 133 us
  matrix products: 108 us -> 0 us
  other arithmetic: 96.8 us -> 5.64 us
  blocking collectives: 63.5 us -> 0 us
  starting transfers between devices: 5.06 us -> 67.7 us
  local copies, waits for them, and re-layouts: 43.9 us -> 28.6 us
    all_gather x4 -> x1, waiting for transfers between devices: 268 us -> 0.01 us  [local(): cot = lax.all_gather(after(cotangent, *toks[1:]), 'x', axis=0, tiled=True)]
    psum x2 -> x0, waiting for transfers between devices: 189 us -> none  [the longest x1 146 us: local(): lax.psum((grad_norm_gain, grad_conv_weight, grad_conv_bias, grad_dt_bias,...]
    pallas_call x0 -> x24, Pallas kernels: none -> 133 us  [call(): pl.pallas_call(body, out_shape=[jax.ShapeDtypeStruct(shape, kind) for sha...]
    ppermute x2 -> x47, waiting for transfers between devices: 3.89 us -> 128 us  [the longest x39 122 us: round_shift(): return lax.ppermute(v, axis, [(s, (s + k) % n) for s in range(n)])]
    dot_general x23 -> x0, matrix products: 108 us -> none  [the longest x3 23.6 us: span_step(): jnp.einsum('tsh,shp->thp', scores[:, :, None] * decay_matrix, scaled_valu...]
    reduce_scatter x2 -> x3, waiting for transfers between devices: 113 us -> 8.33 us  [the longest x1 8.3 us: local(): early = lax.psum_scatter(early, 'z', scatter_dimension=0, tiled=True)]
    ppermute x2 -> x47, starting transfers between devices: 4.52 us -> 67.4 us  [the longest x39 51.8 us: round_shift(): return lax.ppermute(v, axis, [(s, (s + k) % n) for s in range(n)])]
    unnamed x10 -> x4, waiting for transfers between devices: 62.8 us -> 0.57 us
  transfers between devices with their start and end apart: 11 -> 51, of which waited for: 10 -> 27; matrix products, arithmetic and copies ran while one was open for 20% -> 5% of each run, Pallas kernels for 0% -> 22%
where the time goes in v1:
time: 392 us; the launch traced here: 385 us
  waiting for transfers between devices  137 us (35%)
  Pallas kernels  133 us (34%)
  starting transfers between devices  67.7 us (17%)
  local copies, waits for them, and re-layouts  28.6 us (7%)
  between operations  14.4 us (4%)
  other arithmetic  5.64 us (1%)
    pallas_call x24, Pallas kernels, call(): pl.pallas_call(body, out_shape=[jax.ShapeDtypeStruct(shape, kind) for sha...  133 us
    ppermute x39, waiting for transfers between devices, round_shift(): return lax.ppermute(v, axis, [(s, (s + k) % n) for s in range(n)])  122 us
    ppermute x39, starting transfers between devices, round_shift(): return lax.ppermute(v, axis, [(s, (s + k) % n) for s in range(n)])  51.8 us
    unnamed x105, local copies, waits for them, and re-layouts  20.2 us
    ppermute x8, starting transfers between devices, onward(): lax.ppermute(v, 'z', [(s, s + k) for s in range(NZ) if 0 <= s + k < NZ])  15.5 us
    reduce_scatter x1, waiting for transfers between devices, local(): early = lax.psum_scatter(early, 'z', scatter_dimension=0, tiled=True)  8.3 us
  transfers between devices with their start and end apart: 51, of which 27 were waited for; matrix products, arithmetic and copies ran while one was open for 5% of the time, Pallas kernels for 22%

profile of v1, /device:TPU:1, one launch (start us, length us, event | category | flops | bytes accessed | tf_op | source)
XLA Modules:
  0.0 385.4 jit_solution(10903112534271363359)
XLA Ops:
  39.0 7.9 %collective-permute-done.3.t1 = bf16[128,1536]{1,0:T(8,128)(2,1)S(1)} collective-permute-done((bf16[128,1536]{1,0:T(8,128)(2,1)S(1)}, bf16[128,1536]{1,0:T(8,128)(2,1)S(1)}, u32[]{:S(2)}, u32[]{:S(2)}) %collective-permute-start.3) | collective-permute-done | bytes 393248 | tf_op jit(solution)/shard_map/ppermute | solution.py:673
  49.7 16.3 %collective-permute-done.7 = bf16[192,1152]{1,0:T(8,128)(2,1)S(1)} collective-permute-done((bf16[192,1152]{1,0:T(8,128)(2,1)}, bf16[192,1152]{1,0:T(8,128)(2,1)S(1)}, u32[]{:S(2)}, u32[]{:S(2)}) %collective-permute-start.7) | collective-permute-done | bytes 442400 | tf_op jit(solution)/shard_map/ppermute | solution.py:673
  71.9 23.6 %collective-permute-done.17 = bf16[192,1536]{1,0:T(8,128)(2,1)S(1)} collective-permute-done((bf16[192,1536]{1,0:T(8,128)(2,1)S(1)}, bf16[192,1536]{1,0:T(8,128)(2,1)S(1)}, u32[]{:S(2)}, u32[]{:S(2)}) %collective-permute-start.17) | collective-permute-done | bytes 589856 | tf_op jit(solution)/shard_map/ppermute | solution.py:673
  111.6 12.1 %project.1 = (bf16[1536,1152]{1,0:T(8,128)(2,1)}, bf16[528,1024]{1,0:T(8,128)(2,1)}, bf16[512,1024]{1,0:T(8,128)(2,1)}, bf16[512,1024]{1,0:T(8,128)(2,1)}, f32[3...) custom-call(s32[4]{0:T(128)} %pad_add_fusion.idx, bf16[528,1536]{1,0:T(8,128)(2,1)} %get-tuple-element.83.nfull, ...), custom_call_target="tpu_custom_call" | custom-call | flops 6442450944 | bytes 4194304 | tf_op jit(solution)/shard_map/project/pallas_call | solution.py:35
  123.7 4.7 %collective-permute-start.13 = (bf16[144,768]{1,0:T(8,128)(2,1)}, bf16[144,768]{1,0:T(8,128)(2,1)S(1)}, u32[]{:S(2)}, u32[]{:S(2)}) collective-permute-start(bf16[144,768]{1,0:T(8,128)(2,1)} %get-tuple-element.88), channel_id=1, source_target_pairs={{0,12},{1,13},{2,14},{3,15},{16,28},{17,29},{18,30},{19,31},{32,44... | collective-permute-start | bytes 663560 | tf_op jit(solution)/shard_map/ppermute | solution.py:677
  132.3 5.1 %within.1.yi = f32[512,768]{1,0:T(8,128)} custom-call(s32[4]{0:T(128)} %pad_add_fusion.idx, bf16[512,1024]{1,0:T(8,128)(2,1)} %get-tuple-element.85.act, f32[3,512,128]{2,1,0:T(8,128)} %get-tuple-element.86.sm, f32[8,128]{1,0:T(8,128)} %select_maximum_fusion.1.hp), custom_call_target="tpu_custom_call" | custom-call | flops 6442450944 | bytes 4194304 | tf_op jit(solution)/shard_map/within/pallas_call | solution.py:35
  138.8 8.9 %gates.1 = (f32[512,768]{1,0:T(8,128)}, f32[512,768]{1,0:T(8,128)}, bf16[1536,768]{1,0:T(8,128)(2,1)}, bf16[768,1536]{1,0:T(8,128)(2,1)}) custom-call(s32[4]{0:T(128)} %pad_add_fusion.idx, bf16[528,1536]{1,0:T(8,128)(2,1)} %get-tuple-element.83.nfull, bf16[768,1536]{1,0:T(8,128)(2,1)} %constant_dynamic-update-slice_fusion.11.mine, ...), custom_call_target="tpu_custom_call" | custom-call | flops 6442450944 | bytes 4194304 | tf_op jit(solution)/shard_map/gates/pallas_call | solution.py:35
  148.5 7.0 %mix.1 = (f32[512,768]{1,0:T(8,128)}, bf16[4,128,768]{2,1,0:T(8,128)(2,1)}, f32[8,512]{1,0:T(8,128)}) custom-call(s32[4]{0:T(128)} %pad_add_fusion.idx, f32[512,768]{1,0:T(8,128)} %within.1.yi, bf16[512,1024]{1,0:T(8,128)(2,1)} %get-tuple-element.85.act, f32[3,512,128]{2,1,0:T(8,128)} %get-tuple-element.86.sm, f32[4,128,768]{2,1,0:T(8,128)} %get-tuple-element.87.sc, ...), custom_call_target="tpu_custom_call" | custom-call | flops 4294967296 | bytes 4194304 | tf_op jit(solution)/shard_map/mix/pallas_call | solution.py:35
  164.3 10.3 %gated.1 = (bf16[512,768]{1,0:T(8,128)(2,1)}, bf16[512,768]{1,0:T(8,128)(2,1)}, bf16[512,768]{1,0:T(8,128)(2,1)}, bf16[512,1536]{1,0:T(8,128)(2,1)}, bf16[144,768]{1,0:T(8,128)(2,1)}, /*index=5*/f32[8,768]{1,0:T(8,128)}) custom-call(s32[4]{0:T(128)} %pad_add_fusion.idx, f32[512,768]{1,0:T(8,128)} %get-tuple-element.98.mixed, ...), custom_call_target="tpu_custom_call" | custom-call | flops 4294967296 | bytes 4194304 | tf_op jit(solution)/shard_map/gated/pallas_call | solution.py:35
  178.9 8.9 %within_back.1 = (f32[512,768]{1,0:T(8,128)}, f32[512,256]{1,0:T(8,128)}, f32[512,128]{1,0:T(8,128)}) custom-call(s32[4]{0:T(128)} %pad_add_fusion.idx, bf16[512,1024]{1,0:T(8,128)(2,1)} %get-tuple-element.85.act, bf16[512,768]{1,0:T(8,128)(2,1)} %get-tuple-element.102.gmix, f32[3,512,128]{2,1,0:T(8,128)} %get-tuple-element.86.sm), custom_call_target="tpu_custom_call" | custom-call | flops 6442450944 | bytes 4194304 | tf_op jit(solution)/shard_map/within_back/pallas_call | solution.py:35
  189.2 14.1 %across_back.1 = (bf16[528,1152]{1,0:T(8,128)(2,1)}, f32[8,1024]{1,0:T(8,128)}, f32[8,128]{1,0:T(8,128)}) custom-call(s32[4]{0:T(128)} %pad_add_fusion.idx, bf16[512,1024]{1,0:T(8,128)(2,1)} %get-tuple-element.85.act, bf16[512,768]{1,0:T(8,128)(2,1)} %get-tuple-element.102.gmix, f32[3,512,128]{2,1,0:T(8,128)} %get-tuple-element.86.sm, ...), custom_call_target="tpu_custom_call" | custom-call | flops 8589934592 | bytes 4194304 | tf_op jit(solution)/shard_map/across_back/pallas_call | solution.py:35
  203.3 4.4 %late_other.1 = bf16[768,1152]{1,0:T(8,128)(2,1)} custom-call(s32[4]{0:T(128)} %pad_add_fusion.idx, bf16[528,1152]{1,0:T(8,128)(2,1)} %get-tuple-element.110.gpa, bf16[768,528]{1,0:T(8,128)(2,1)} %get-tuple-element.119.turned), custom_call_target="tpu_custom_call" | custom-call | flops 2147483648 | bytes 4194304 | tf_op jit(solution)/shard_map/late_other/pallas_call | solution.py:35
  214.6 5.0 %late_mine.1 = bf16[768,1152]{1,0:T(8,128)(2,1)} custom-call(s32[4]{0:T(128)} %pad_add_fusion.idx, bf16[528,1152]{1,0:T(8,128)(2,1)} %get-tuple-element.110.gpa, bf16[768,528]{1,0:T(8,128)(2,1)} %get-tuple-element.118.turned, bf16[768,1152]{1,0:T(8,128)(2,1)} %copy-done.33), custom_call_target="tpu_custom_call" | custom-call | flops 2147483648 | bytes 4194304 | tf_op jit(solution)/shard_map/late_mine/pallas_call | solution.py:35
  219.9 6.3 %early_other.1 = bf16[768,1536]{1,0:T(8,128)(2,1)} custom-call(s32[4]{0:T(128)} %pad_add_fusion.idx, bf16[512,768]{1,0:T(8,128)(2,1)} %get-tuple-element.120.ny, bf16[512,1536]{1,0:T(8,128)(2,1)} %all-gather.2.cloned.1.call-done.cot, bf16[512,768]{1,0:T(8,128)(2,1)} %get-tuple-element.111.ggate, bf16[768,528]{1,0:T(8,128)(2,1)} %get-tuple-element.119.turned), custom_call_target="tpu_custom_call" | custom-call | flops 3221225472 | bytes 4194304 | tf_op jit(solution)/shard_map/early_other/pallas_call | solution.py:35
  232.3 7.7 %early_mine.1 = bf16[768,1536]{1,0:T(8,128)(2,1)} custom-call(s32[4]{0:T(128)} %pad_add_fusion.idx, bf16[512,768]{1,0:T(8,128)(2,1)} %get-tuple-element.120.ny, bf16[512,1536]{1,0:T(8,128)(2,1)} %all-gather.2.cloned.1.call-done.cot, bf16[512,768]{1,0:T(8,128)(2,1)} %get-tuple-element.111.ggate, bf16[768,528]{1,0:T(8,128)(2,1)} %get-tuple-element.118.turned, ...), custom_call_target="tpu_custom_call" | custom-call | flops 3221225472 | bytes 4194304 | tf_op jit(solution)/shard_map/early_mine/pallas_call | solution.py:35
  246.0 4.6 %collective-permute-done.27.rim = bf16[16,1536]{1,0:T(8,128)(2,1)S(1)} collective-permute-done((bf16[16,1536]{1,0:T(8,128)(2,1)}, bf16[16,1536]{1,0:T(8,128)(2,1)S(1)}, u32[]{:S(2)}, u32[]{:S(2)}) %collective-permute-start.27) | collective-permute-done | bytes 49184 | tf_op jit(solution)/shard_map/ppermute | solution.py:677
  251.2 9.9 %normed_back.1 = (f32[128,1536]{1,0:T(8,128)}, bf16[128,1536]{1,0:T(8,128)(2,1)}, bf16[128,1536]{1,0:T(8,128)(2,1)}, bf16[128,1536]{1,0:T(8,128)(2,1)}, f32[8,1536]{1,0:T(8,128)}) custom-call(s32[4]{0:T(128)} %pad_add_fusion.idx, bf16[528,1152]{1,0:T(8,128)(2,1)} %get-tuple-element.110.gpa, bf16[512,768]{1,0:T(8,128)(2,1)} %get-tuple-element.111.ggate, ...), custom_call_target="tpu_custom_call" | custom-call | flops 4294967296 | bytes 4194304 | tf_op jit(solution)/shard_map/normed_back/pallas_call | solution.py:35
  276.7 8.3 %reduce-scatter.8.cloned.1.call-done.early = bf16[192,1536]{1,0:T(8,128)(2,1)} async-done(((bf16[768,1536]{1,0:T(8,128)(2,1)}), bf16[192,1536]{1,0:T(8,128)(2,1)}) %reduce-scatter.8.cloned.1.call-update) | async-done | bytes 589840 | tf_op jit(solution)/shard_map/reduce_scatter | solution.py:801
  292.6 5.2 %collective-permute-done.37.b = bf16[320,512]{1,0:T(8,128)(2,1)S(1)} collective-permute-done((bf16[320,512]{1,0:T(8,128)(2,1)}, bf16[320,512]{1,0:T(8,128)(2,1)S(1)}, u32[]{:S(2)}, u32[]{:S(2)}) %collective-permute-start.37) | collective-permute-done | bytes 327712 | tf_op jit(solution)/shard_map/ppermute | solution.py:673
  297.8 8.0 %collective-permute-done.38.c = bf16[320,512]{1,0:T(8,128)(2,1)S(1)} collective-permute-done((bf16[320,512]{1,0:T(8,128)(2,1)}, bf16[320,512]{1,0:T(8,128)(2,1)S(1)}, u32[]{:S(2)}, u32[]{:S(2)}) %collective-permute-start.38) | collective-permute-done | bytes 327712 | tf_op jit(solution)/shard_map/ppermute | solution.py:673
  323.2 6.2 %collective-permute-done.45.d = bf16[288,512]{1,0:T(8,128)(2,1)S(1)} collective-permute-done((bf16[288,512]{1,0:T(8,128)(2,1)}, bf16[288,512]{1,0:T(8,128)(2,1)S(1)}, u32[]{:S(2)}, u32[]{:S(2)}) %collective-permute-start.45) | collective-permute-done | bytes 294944 | tf_op jit(solution)/shard_map/ppermute | solution.py:673
  331.1 8.4 %collective-permute-done.43.b = bf16[288,512]{1,0:T(8,128)(2,1)S(1)} collective-permute-done((bf16[288,512]{1,0:T(8,128)(2,1)}, bf16[288,512]{1,0:T(8,128)(2,1)S(1)}, u32[]{:S(2)}, u32[]{:S(2)}) %collective-permute-start.43) | collective-permute-done | bytes 294944 | tf_op jit(solution)/shard_map/ppermute | solution.py:673
  345.6 8.5 %collective-permute-done.28.g1 = bf16[128,1536]{1,0:T(8,128)(2,1)S(1)} collective-permute-done((bf16[128,1536]{1,0:T(8,128)(2,1)S(1)}, bf16[128,1536]{1,0:T(8,128)(2,1)S(1)}, u32[]{:S(2)}, u32[]{:S(2)}) %collective-permute-start.28) | collective-permute-done | bytes 393248 | tf_op jit(solution)/shard_map/ppermute | solution.py:673
  354.1 8.7 %collective-permute-done.29.g2 = bf16[128,1536]{1,0:T(8,128)(2,1)S(1)} collective-permute-done((bf16[128,1536]{1,0:T(8,128)(2,1)S(1)}, bf16[128,1536]{1,0:T(8,128)(2,1)S(1)}, u32[]{:S(2)}, u32[]{:S(2)}) %collective-permute-start.29) | collective-permute-done | bytes 393248 | tf_op jit(solution)/shard_map/ppermute | solution.py:673
  (254 shorter events, 160.8 us)
Async XLA Ops:
  7.2 130.2 %all-gather.2.cloned.1.call-start = ((), (), s32[]{:S(2)}) async-start(), calls=%async_computation.3 | async-start | bytes 1966080 | tf_op jit(solution)/shard_map/all_gather | solution.py:739
  11.9 17.5 %collective-permute-start.14 = (bf16[48,768]{1,0:T(8,128)(2,1)}, bf16[48,768]{1,0:T(8,128)(2,1)S(1)}, u32[]{:S(2)}, u32[]{:S(2)}) collective-permute-start(bf16[48,768]{1,0:T(8,128)(2,1)} %get-tuple-element.91), channel_id=1, source_target_pairs={{0,1},{1,2},{2,3},{3,0},{4,5},{5,6},{6,7},{7,4},{8,9},{9,10},{10,1... | collective-permute-start | bytes 221192 | tf_op jit(solution)/shard_map/ppermute | solution.py:673
  13.9 34.7 %collective-permute-start.15 = (bf16[48,768]{1,0:T(8,128)(2,1)}, bf16[48,768]{1,0:T(8,128)(2,1)}, u32[]{:S(2)}, u32[]{:S(2)}) collective-permute-start(bf16[48,768]{1,0:T(8,128)(2,1)} %get-tuple-element.92), channel_id=1, source_target_pairs={{0,2},{1,3},{2,0},{3,1},{4,6},{5,7},{6,4},{7,5},{8,10},{9,11},{10,... | collective-permute-start | bytes 221192 | tf_op jit(solution)/shard_map/ppermute | solution.py:673
  27.3 19.6 %collective-permute-start.3 = (bf16[128,1536]{1,0:T(8,128)(2,1)S(1)}, bf16[128,1536]{1,0:T(8,128)(2,1)S(1)}, u32[]{:S(2)}, u32[]{:S(2)}) collective-permute-start(bf16[128,1536]{1,0:T(8,128)(2,1)S(1)} %copy-done.2), channel_id=1, source_target_pairs={{0,1},{1,2},{2,3},{3,0},{4,5},{5,6},{6,7},{7,4},{8,9},{9,10},{10,1... | collective-permute-start | bytes 1179656 | tf_op jit(solution)/shard_map/ppermute | solution.py:673
  29.4 19.2 %collective-permute-start.16 = (bf16[48,768]{1,0:T(8,128)(2,1)}, bf16[48,768]{1,0:T(8,128)(2,1)}, u32[]{:S(2)}, u32[]{:S(2)}) collective-permute-start(bf16[48,768]{1,0:T(8,128)(2,1)} %get-tuple-element.93), channel_id=1, source_target_pairs={{0,3},{1,0},{2,1},{3,2},{4,7},{5,4},{6,5},{7,6},{8,11},{9,8},{10,9... | collective-permute-start | bytes 221192 | tf_op jit(solution)/shard_map/ppermute | solution.py:673
  33.9 15.8 %collective-permute-start.9 = (bf16[192,1152]{1,0:T(8,128)(2,1)}, bf16[192,1152]{1,0:T(8,128)(2,1)S(1)}, u32[]{:S(2)}, u32[]{:S(2)}) collective-permute-start(bf16[192,1152]{1,0:T(8,128)(2,1)} %get-tuple-element.166), channel_id=1, source_target_pairs={{0,12},{4,0},{8,4},{12,8},{1,13},{5,1},{9,5},{13,9},{2,14},{6,2},{... | collective-permute-start | bytes 1327112 | tf_op jit(solution)/shard_map/ppermute | solution.py:673
  46.9 19.2 %collective-permute-start.7 = (bf16[192,1152]{1,0:T(8,128)(2,1)}, bf16[192,1152]{1,0:T(8,128)(2,1)S(1)}, u32[]{:S(2)}, u32[]{:S(2)}) collective-permute-start(bf16[192,1152]{1,0:T(8,128)(2,1)} %get-tuple-element.166), channel_id=1, source_target_pairs={{0,4},{4,8},{8,12},{12,0},{1,5},{5,9},{9,13},{13,1},{2,6},{6,10},{... | collective-permute-start | bytes 1327112 | tf_op jit(solution)/shard_map/ppermute | solution.py:673
  48.6 228.2 %reduce-scatter.6.cloned.1.call-start = ((), (), s32[]{:S(2)}) async-start(), calls=%async_computation.5 | async-start | bytes 2211840 | tf_op jit(solution)/shard_map/reduce_scatter | solution.py:815
  66.0 31.1 %collective-permute-start.19 = (bf16[192,1536]{1,0:T(8,128)(2,1)S(1)}, bf16[192,1536]{1,0:T(8,128)(2,1)S(1)}, u32[]{:S(2)}, u32[]{:S(2)}) collective-permute-start(bf16[192,1536]{1,0:T(8,128)(2,1)S(1)} %maximum_maximum_fusion), channel_id=1, source_target_pairs={{0,12},{4,0},{8,4},{12,8},{1,13},{5,1},{9,5},{13,9},{2,14},{6,2},{... | collective-permute-start | bytes 1769480 | tf_op jit(solution)/shard_map/ppermute | solution.py:673
  66.0 30.3 %collective-permute-start.18 = (bf16[192,1536]{1,0:T(8,128)(2,1)S(1)}, bf16[192,1536]{1,0:T(8,128)(2,1)S(1)}, u32[]{:S(2)}, u32[]{:S(2)}) collective-permute-start(bf16[192,1536]{1,0:T(8,128)(2,1)S(1)} %maximum_maximum_fusion), channel_id=1, source_target_pairs={{0,8},{4,12},{8,0},{12,4},{1,9},{5,13},{9,1},{13,5},{2,10},{6,14},... | collective-permute-start | bytes 1769480 | tf_op jit(solution)/shard_map/ppermute | solution.py:673
  66.0 29.4 %collective-permute-start.17 = (bf16[192,1536]{1,0:T(8,128)(2,1)S(1)}, bf16[192,1536]{1,0:T(8,128)(2,1)S(1)}, u32[]{:S(2)}, u32[]{:S(2)}) collective-permute-start(bf16[192,1536]{1,0:T(8,128)(2,1)S(1)} %maximum_maximum_fusion), channel_id=1, source_target_pairs={{0,4},{4,8},{8,12},{12,0},{1,5},{5,9},{9,13},{13,1},{2,6},{6,10},{... | collective-permute-start | bytes 1769480 | tf_op jit(solution)/shard_map/ppermute | solution.py:673
  70.9 40.7 %collective-permute-start.10 = (bf16[768,1152]{1,0:T(8,128)(2,1)}, bf16[768,1152]{1,0:T(8,128)(2,1)}, u32[]{:S(2)}, u32[]{:S(2)}) collective-permute-start(bf16[768,1152]{1,0:T(8,128)(2,1)} %constant_dynamic-update-slice_fusion.4.mine), channel_id=1, source_target_pairs={{0,16},{16,0},{1,17},{17,1},{2,18},{18,2},{3,19},{19,3},{4,20},{20... | collective-permute-start | bytes 5308424 | tf_op jit(solution)/shard_map/ppermute | solution.py:673
  98.0 39.4 %collective-permute-start.20 = (bf16[768,1536]{1,0:T(8,128)(2,1)}, bf16[768,1536]{1,0:T(8,128)(2,1)S(1)}, u32[]{:S(2)}, u32[]{:S(2)}) collective-permute-start(bf16[768,1536]{1,0:T(8,128)(2,1)} %constant_dynamic-update-slice_fusion.11.mine), channel_id=1, source_target_pairs={{0,16},{16,0},{1,17},{17,1},{2,18},{18,2},{3,19},{19,3},{4,20},{20... | collective-permute-start | bytes 7077896 | tf_op jit(solution)/shard_map/ppermute | solution.py:673
  123.7 24.0 %collective-permute-start.13 = (bf16[144,768]{1,0:T(8,128)(2,1)}, bf16[144,768]{1,0:T(8,128)(2,1)S(1)}, u32[]{:S(2)}, u32[]{:S(2)}) collective-permute-start(bf16[144,768]{1,0:T(8,128)(2,1)} %get-tuple-element.88), channel_id=1, source_target_pairs={{0,12},{1,13},{2,14},{3,15},{16,28},{17,29},{18,30},{19,31},{32,44... | collective-permute-start | bytes 663560 | tf_op jit(solution)/shard_map/ppermute | solution.py:677
  128.5 19.2 %collective-permute-start.12 = (bf16[144,768]{1,0:T(8,128)(2,1)}, bf16[144,768]{1,0:T(8,128)(2,1)S(1)}, u32[]{:S(2)}, u32[]{:S(2)}) collective-permute-start(bf16[144,768]{1,0:T(8,128)(2,1)} %get-tuple-element.88), channel_id=1, source_target_pairs={{0,8},{4,12},{1,9},{5,13},{2,10},{6,14},{3,11},{7,15},{16,24},{20,... | collective-permute-start | bytes 663560 | tf_op jit(solution)/shard_map/ppermute | solution.py:677
  129.8 17.9 %collective-permute-start.11 = (bf16[144,768]{1,0:T(8,128)(2,1)}, bf16[144,768]{1,0:T(8,128)(2,1)S(1)}, u32[]{:S(2)}, u32[]{:S(2)}) collective-permute-start(bf16[144,768]{1,0:T(8,128)(2,1)} %get-tuple-element.88), channel_id=1, source_target_pairs={{0,4},{4,8},{8,12},{1,5},{5,9},{9,13},{2,6},{6,10},{10,14},{3,7},{... | collective-permute-start | bytes 663560 | tf_op jit(solution)/shard_map/ppermute | solution.py:677
  219.7 65.3 %reduce-scatter.8.cloned.1.call-start = ((), (), s32[]{:S(2)}) async-start(), calls=%async_computation.6 | async-start | bytes 2949120 | tf_op jit(solution)/shard_map/reduce_scatter | solution.py:801
  240.0 126.9 %reduce-scatter.4.cloned.1.call-start = ((), (), s32[]{:S(2)}) async-start(), calls=%async_computation.4 | async-start | bytes 1966080 | tf_op jit(solution)/shard_map/reduce_scatter | solution.py:802
  289.0 16.8 %collective-permute-start.38 = (bf16[320,512]{1,0:T(8,128)(2,1)}, bf16[320,512]{1,0:T(8,128)(2,1)S(1)}, u32[]{:S(2)}, u32[]{:S(2)}) collective-permute-start(bf16[320,512]{1,0:T(8,128)(2,1)} %get-tuple-element.127), channel_id=1, source_target_pairs={{0,64},{32,96},{64,0},{96,32},{1,65},{33,97},{65,1},{97,33},{2,66}... | collective-permute-start | bytes 983048 | tf_op jit(solution)/shard_map/ppermute | solution.py:673
  291.4 14.4 %collective-permute-start.39 = (bf16[320,512]{1,0:T(8,128)(2,1)}, bf16[320,512]{1,0:T(8,128)(2,1)S(1)}, u32[]{:S(2)}, u32[]{:S(2)}) collective-permute-start(bf16[320,512]{1,0:T(8,128)(2,1)} %get-tuple-element.128), channel_id=1, source_target_pairs={{0,96},{32,0},{64,32},{96,64},{1,97},{33,1},{65,33},{97,65},{2,98}... | collective-permute-start | bytes 983048 | tf_op jit(solution)/shard_map/ppermute | solution.py:673
  323.0 16.5 %collective-permute-start.43 = (bf16[288,512]{1,0:T(8,128)(2,1)}, bf16[288,512]{1,0:T(8,128)(2,1)S(1)}, u32[]{:S(2)}, u32[]{:S(2)}) collective-permute-start(bf16[288,512]{1,0:T(8,128)(2,1)} %get-tuple-element.135.a), channel_id=1, source_target_pairs={{0,32},{32,64},{64,96},{96,0},{1,33},{33,65},{65,97},{97,1},{2,34}... | collective-permute-start | bytes 884744 | tf_op jit(solution)/shard_map/ppermute | solution.py:673
  341.7 30.4 %collective-permute-start.46 = (bf16[1152,512]{1,0:T(8,128)(2,1)}, bf16[1152,512]{1,0:T(8,128)(2,1)S(1)}, u32[]{:S(2)}, u32[]{:S(2)}) collective-permute-start(bf16[1152,512]{1,0:T(8,128)(2,1)} %pad_maximum_fusion), channel_id=1, source_target_pairs={{0,16},{16,0},{1,17},{17,1},{2,18},{18,2},{3,19},{19,3},{4,20},{20... | collective-permute-start | bytes 3538952 | tf_op jit(solution)/shard_map/ppermute | solution.py:673
  342.2 20.6 %collective-permute-start.29 = (bf16[128,1536]{1,0:T(8,128)(2,1)S(1)}, bf16[128,1536]{1,0:T(8,128)(2,1)S(1)}, u32[]{:S(2)}, u32[]{:S(2)}) collective-permute-start(bf16[128,1536]{1,0:T(8,128)(2,1)S(1)} %copy-done.35), channel_id=1, source_target_pairs={{0,2},{1,3},{2,0},{3,1},{4,6},{5,7},{6,4},{7,5},{8,10},{9,11},{10,... | collective-permute-start | bytes 1179656 | tf_op jit(solution)/shard_map/ppermute | solution.py:673
  345.1 17.7 %collective-permute-start.30 = (bf16[128,1536]{1,0:T(8,128)(2,1)S(1)}, bf16[128,1536]{1,0:T(8,128)(2,1)S(1)}, u32[]{:S(2)}, u32[]{:S(2)}) collective-permute-start(bf16[128,1536]{1,0:T(8,128)(2,1)S(1)} %copy-done.34), channel_id=1, source_target_pairs={{0,3},{1,0},{2,1},{3,2},{4,7},{5,4},{6,5},{7,6},{8,11},{9,8},{10,9... | collective-permute-start | bytes 1179656 | tf_op jit(solution)/shard_map/ppermute | solution.py:673
  (79 other events, 917.3 us)
Sparse Core Ops, SparseCore 0:
  48.7 28.0 all-gather.1
  219.8 29.5 reduce-scatter.5
  252.0 33.0 reduce-scatter.7
  287.4 24.1 reduce-scatter.3
